TPU v7x, 256 devices: a whole 4x4x8 slice. The times are simulated.
256 devices in a mesh: group: 4 (over y), dev: 64 (over z, x, core).
Axes of the slice: x: 4, y: 4, z: 8, core: 2. Of those that a mesh axis runs over, the one named last changes fastest.
Arguments:
- tokens: bfloat16 [32768, 5120], P(('group', 'dev')), may hold values from -6 to 6
- cotangent: bfloat16 [32768, 5120], P(('group', 'dev')), may hold values from -6 to 6
- routes: int32 [32768, 1], P(('group', 'dev')), may hold values from 0 to 7; in each aligned block of 128 rows (0 to 127, 128 to 255, ...) at most 20 rows name the same one
- codes: bfloat16 [3, 6144, 5120], P(None, 'dev', 'group'), may hold values from -0.078125 to 0.078125
- scales: float32 [3, 6144, 40], P(None, 'dev', 'group'), may hold values from 0.5 to 2
- first_moment: float32 [3, 6144, 5120], P(None, 'dev', 'group'), may hold values from -18 to 18
- second_moment: float32 [3, 6144, 5120], P(None, 'dev', 'group'), may hold values from 0.2 to 5
Outputs:
- grad_tokens: bfloat16 [32768, 5120], P(('group', 'dev'))
- new_weights: float32 [3, 6144, 5120], P(None, 'dev', 'group')
- new_first: float32 [3, 6144, 5120], P(None, 'dev', 'group')
- new_second: float32 [3, 6144, 5120], P(None, 'dev', 'group')
Inputs may be any that keep to these rules, and one draw needn't show every extreme that they name: `routes`: among the rows of one device, no expert is named by more than 20 rows; in every draw some expert is named by exactly 20 rows of some device.
All inputs are finite; a program needn't handle non-finite values.
Results may differ from a plain program's by a relative error of at most 0.018.
Values may be sent and summed in bfloat16 or wider, within the bound.
A program may use at most 128 MiB of HBM per device.

v0:
```python
import jax
import jax.numpy as jnp
from jax import lax
from jax.sharding import PartitionSpec as P

SLICES = 4
COPIES = 2
QB = 128


BETA_ONE = 0.9
BETA_TWO = 0.999
LEARNING_RATE = 0.01
ADAM_EPS = 1e-08
STEP_COUNT = 10


def partner_2(block, axis, apart):
    count = lax.axis_size(axis)
    route = []
    for low in range(count):
        high = low | 1 << apart
        if high != low and high < count:
            route += [(low, high), (high, low)]
    return lax.ppermute(block, axis, route)


def contract_rows(first_op, second_op):
    return lax.dot_general(
        first_op, second_op, (((0,), (0,)), ((), ())), preferred_element_type=jnp.float32
    )


def contract_cols(first_op, second_op):
    return lax.dot_general(
        first_op, second_op, (((1,), (1,)), ((), ())), preferred_element_type=jnp.float32
    )


def round_trip(values):
    return lax.optimization_barrier(values.astype(jnp.bfloat16)).astype(jnp.float32)


def shards(tokens, cotangent, routes, codes, scales, first_moment, second_moment):
    row_count, feature_count = tokens.shape
    device_count = lax.axis_size("dev")
    expert_count = device_count // (SLICES * COPIES)
    capacity = COPIES * min(row_count // COPIES, 5 * row_count // (8 * expert_count))
    half_slots = capacity // COPIES
    dev_position = lax.axis_index("dev")
    lower_copy = dev_position & 1 == 0
    owned_full = codes.astype(jnp.float32) * jnp.repeat(scales, QB, axis=2)
    owned = owned_full.astype(jnp.bfloat16)
    gathered = lax.all_gather(owned, "group", axis=2, tiled=True)
    partner = partner_2(gathered, "dev", 0)
    weights = jnp.where(
        lower_copy,
        jnp.concatenate([gathered, partner], axis=1),
        jnp.concatenate([partner, gathered], axis=1),
    )
    gate_weight = weights[0]
    upward_weight = weights[1]
    down_weight = weights[2]
    route_ids = routes[:, 0]
    matches = route_ids[:, None] == jnp.arange(expert_count, dtype=jnp.int32)[None, :]
    counted = matches.astype(jnp.int32)
    earlier = jnp.cumsum(counted, axis=0) - counted
    target = route_ids * capacity + jnp.sum(jnp.where(matches, earlier, 0), axis=1)
    slot_range = jnp.arange(expert_count * capacity, dtype=jnp.int32)
    dispatch = (target[:, None] == slot_range[None, :]).astype(jnp.bfloat16)
    packed = contract_rows(dispatch, jnp.concatenate([tokens, cotangent], axis=1)).astype(
        jnp.bfloat16
    )
    send_rows = packed[:, :feature_count].reshape(expert_count, COPIES, half_slots, feature_count)
    send_cot = packed[:, feature_count:].reshape(expert_count, COPIES, half_slots, feature_count)

    def replicate(values):
        spread = jnp.broadcast_to(
            values[:, None], (expert_count, SLICES, COPIES, half_slots, feature_count)
        )
        return spread.reshape(expert_count * SLICES * COPIES * half_slots, feature_count)

    inbound, cot_inbound = (
        lax.all_to_all(replicate(send_rows), "dev", split_axis=0, concat_axis=0, tiled=True),
        lax.all_to_all(replicate(send_cot), "dev", split_axis=0, concat_axis=0, tiled=True),
    )
    gate_proj = contract_cols(inbound, gate_weight)
    upward = contract_cols(inbound, upward_weight)
    sigmoid_gate = jax.nn.sigmoid(gate_proj)
    activated = gate_proj * sigmoid_gate
    hidden = (activated * upward).astype(jnp.bfloat16)
    hidden_cot = contract_cols(cot_inbound, down_weight)
    down_grad = round_trip(contract_rows(hidden, cot_inbound))
    gate_cot = (
        hidden_cot * upward * sigmoid_gate * (1.0 + gate_proj * (1.0 - sigmoid_gate))
    ).astype(jnp.bfloat16)
    upward_cot = (hidden_cot * activated).astype(jnp.bfloat16)
    gate_grad = round_trip(contract_rows(gate_cot, inbound))
    upward_grad = round_trip(contract_rows(upward_cot, inbound))
    partial_term = (
        jnp.dot(gate_cot, gate_weight, preferred_element_type=jnp.float32)
        + jnp.dot(upward_cot, upward_weight, preferred_element_type=jnp.float32)
    ).astype(jnp.bfloat16)
    shares = lax.psum_scatter(
        jnp.stack([gate_grad, upward_grad, down_grad]).astype(jnp.bfloat16),
        "group",
        scatter_dimension=2,
        tiled=True,
    ).astype(jnp.float32)
    stored = shares.shape[1] // COPIES
    kept = jnp.where(lower_copy, shares[:, :stored], shares[:, stored:])
    given = jnp.where(lower_copy, shares[:, stored:], shares[:, :stored])
    gradient = kept + partner_2(given.astype(jnp.bfloat16), "dev", 0).astype(given.dtype)
    returned = lax.all_to_all(partial_term, "dev", split_axis=0, concat_axis=0, tiled=True)
    layered = returned.astype(jnp.float32).reshape(
        expert_count, SLICES, COPIES, half_slots, feature_count
    )
    summed = jnp.sum(layered, axis=1).reshape(expert_count * capacity, feature_count)
    rounded_sums = summed.astype(jnp.bfloat16)
    grad_tokens = jnp.dot(dispatch, rounded_sums, preferred_element_type=jnp.float32).astype(
        jnp.bfloat16
    )
    new_first = BETA_ONE * first_moment + (1.0 - BETA_ONE) * gradient
    new_second = BETA_TWO * second_moment + (1.0 - BETA_TWO) * gradient * gradient
    first_fix = 1.0 - BETA_ONE**STEP_COUNT
    second_fix = 1.0 - BETA_TWO**STEP_COUNT
    new_weights = owned_full - LEARNING_RATE * (new_first / first_fix) / (
        jnp.sqrt(new_second / second_fix) + ADAM_EPS
    )
    return (grad_tokens, new_weights, new_first, new_second)


def solution(mesh):
    in_specs = (
        P(("group", "dev"), None),
        P(("group", "dev"), None),
        P(("group", "dev"), None),
        P(None, "dev", "group"),
        P(None, "dev", "group"),
        P(None, "dev", "group"),
        P(None, "dev", "group"),
    )
    out_specs = (
        P(("group", "dev"), None),
        P(None, "dev", "group"),
        P(None, "dev", "group"),
        P(None, "dev", "group"),
    )
    return jax.shard_map(shards, mesh=mesh, in_specs=in_specs, out_specs=out_specs, check_vma=False)
```

profile of v0, /device:TPU:1, one launch (start us, length us, event | category | flops | bytes accessed | tf_op | source)
XLA Modules:
  0.0 820.3 jit_solution(8290986392239907254)
XLA Ops:
  7.2 0.7 fusion.13
  7.9 0.2 reduce_window_sum.11
  8.1 0.8 select_reduce_fusion
  8.9 0.7 fusion.14
  9.6 2.8 convolution_convert_fusion
  12.4 1.9 fusion.18
  14.3 2.5 broadcast_in_dim.28
  16.9 5.1 broadcast_in_dim.29
  22.0 13.2 %all-to-all-start.1 = ((bf16[64,10,5120]{2,1,0:T(8,128)(2,1)}), bf16[64,10,5120]{2,1,0:T(8,128)(2,1)}, u32[]{:S(2)}, u32[]{:S(2)}) async-start(bf16[64,10,5120]{2,1,0:T(8,128)(2,1)} %bitcast.39), calls=%async_computation.1 | async-start | bytes 20971520 | tf_op jit(solution)/shard_map/all_to_all | solution.py:84
  35.2 2.5 broadcast_in_dim.25
  37.7 227.2 %all-to-all-done.1 = bf16[64,10,5120]{2,1,0:T(8,128)(2,1)} async-done(((bf16[64,10,5120]{2,1,0:T(8,128)(2,1)}), bf16[64,10,5120]{2,1,0:T(8,128)(2,1)}, u32[]{:S(2)}, u32[]{:S(2)}) %all-to-all-start.1) | async-done | bytes 6553632 | tf_op jit(solution)/shard_map/all_to_all | solution.py:84
  264.9 5.3 broadcast_in_dim.26
  270.2 9.8 %all-to-all-start = ((bf16[64,10,5120]{2,1,0:T(8,128)(2,1)}), bf16[64,10,5120]{2,1,0:T(8,128)(2,1)}, u32[]{:S(2)}, u32[]{:S(2)}) async-start(bf16[64,10,5120]{2,1,0:T(8,128)(2,1)} %bitcast.38), calls=%async_computation | async-start | bytes 20971520 | tf_op jit(solution)/shard_map/all_to_all | solution.py:85
  280.0 0.0 all-gather.2.cloned.1.call-start
  280.1 0.1 broadcast_in_dim.27
  280.2 0.8 copy.13
  281.0 2.1 fusion.8
  283.2 0.0 all-gather.2.cloned.1.call-update
  283.2 0.0 reduce-scatter.2.cloned.1.call-start
  283.2 41.7 %all-gather.2.cloned.1.call-done = bf16[3,96,5120]{2,1,0:T(8,128)(2,1)} async-done(((bf16[3,96,1280]{2,1,0:T(8,128)(2,1)}), bf16[3,96,5120]{2,1,0:T(8,128)(2,1)}) %all-gather.2.cloned.1.call-update) | async-done | bytes 2949136 | tf_op jit(solution)/shard_map/all_gather | solution.py:54
  324.9 0.7 collective-permute-start
  325.6 5.3 collective-permute-done
  331.0 9.6 %maximum_select_fusion = bf16[3,192,5120]{2,1,0:T(8,128)(2,1)} fusion(bf16[3,96,5120]{2,1,0:T(8,128)(2,1)} %collective-permute-done, bf16[3,96,5120]{2,1,0:T(8,128)(2,1)} %all-gather.2.cloned.1.call-done, pred[]{:T(512)S(6)} %eq.41), kind=kLoop, calls=%fused_computation.6 | loop fusion | flops 26542080 | bytes 11796481 | tf_op jit(solution)/shard_map/jit(_where)/select_n | solution.py:56
  340.6 12.9 %all_to_all.27 = bf16[640,5120]{1,0:T(8,128)(2,1)} reshape(bf16[64,10,5120]{2,1,0:T(8,128)(2,1)} %all-to-all-done.1) | data formatting | bytes 13107200 | tf_op jit(solution)/shard_map/all_to_all | solution.py:84
  353.5 5.9 fusion.6
  359.4 3.9 fusion.4
  363.3 146.5 %all-to-all-done = bf16[64,10,5120]{2,1,0:T(8,128)(2,1)} async-done(((bf16[64,10,5120]{2,1,0:T(8,128)(2,1)}), bf16[64,10,5120]{2,1,0:T(8,128)(2,1)}, u32[]{:S(2)}, u32[]{:S(2)}) %all-to-all-start) | async-done | bytes 6553632 | tf_op jit(solution)/shard_map/all_to_all | solution.py:85
  509.7 12.9 %all_to_all.24 = bf16[640,5120]{1,0:T(8,128)(2,1)} reshape(bf16[64,10,5120]{2,1,0:T(8,128)(2,1)} %all-to-all-done) | data formatting | bytes 13107200 | tf_op jit(solution)/shard_map/all_to_all | solution.py:85
  522.6 5.9 multiply_convert_fusion.1
  528.6 1.7 convolution_convert_fusion.1
  530.3 4.6 convolution_convert_fusion.2
  534.9 1.8 convolution_convert_fusion.3
  536.7 3.1 pad_maximum_fusion
  539.8 0.0 reduce-scatter.2.cloned.1.call-update
  539.8 3.4 fusion.5
  543.2 6.2 add_convert_fusion
  549.5 12.7 %all_to_all.28 = bf16[64,10,5120]{2,1,0:T(8,128)(2,1)} reshape(bf16[640,5120]{1,0:T(8,128)(2,1)} %add_convert_fusion) | data formatting | bytes 13107200 | tf_op jit(solution)/shard_map/all_to_all | solution.py:114
  562.2 10.3 %all-to-all-start.2 = ((bf16[64,10,5120]{2,1,0:T(8,128)(2,1)}), bf16[64,10,5120]{2,1,0:T(8,128)(2,1)}, u32[]{:S(2)}, u32[]{:S(2)}) async-start(bf16[64,10,5120]{2,1,0:T(8,128)(2,1)} %all_to_all.28), calls=%async_computation.2 | async-start | bytes 20971520 | tf_op jit(solution)/shard_map/all_to_all | solution.py:114
  572.5 31.2 %reduce-scatter.2.cloned.1.call-done = bf16[3,192,1280]{2,1,0:T(8,128)(2,1)} async-done(((bf16[3,192,5120]{2,1,0:T(8,128)(2,1)}), bf16[3,192,1280]{2,1,0:T(8,128)(2,1)}) %reduce-scatter.2.cloned.1.call-update) | async-done | bytes 1474576 | tf_op jit(solution)/shard_map/reduce_scatter | solution.py:104
  603.7 1.8 convert_element_type.79
  605.4 0.1 select_convert_fusion
  605.6 0.7 collective-permute-start.1
  606.3 1.8 collective-permute-done.1
  608.1 2.9 divide_subtract_fusion
  611.0 191.2 %all-to-all-done.2 = bf16[64,10,5120]{2,1,0:T(8,128)(2,1)} async-done(((bf16[64,10,5120]{2,1,0:T(8,128)(2,1)}), bf16[64,10,5120]{2,1,0:T(8,128)(2,1)}, u32[]{:S(2)}, u32[]{:S(2)}) %all-to-all-start.2) | async-done | bytes 6553632 | tf_op jit(solution)/shard_map/all_to_all | solution.py:114
  802.2 6.2 reduce
  808.4 2.0 convert_element_type.73
  810.5 3.0 convolution_convert_fusion.4
  (18 shorter events, 0.0 us)
Async XLA Ops:
  22.0 242.9 %all-to-all-start.1 = ((bf16[64,10,5120]{2,1,0:T(8,128)(2,1)}), bf16[64,10,5120]{2,1,0:T(8,128)(2,1)}, u32[]{:S(2)}, u32[]{:S(2)}) async-start(bf16[64,10,5120]{2,1,0:T(8,128)(2,1)} %bitcast.39), calls=%async_computation.1 | async-start | bytes 20971520 | tf_op jit(solution)/shard_map/all_to_all | solution.py:84
  270.2 9.9 %copy-start.5 = (f32[3,96,10]{1,0,2:T(4,128)S(1)}, f32[3,96,10]{1,0,2:T(4,128)}, u32[]{:S(2)}) copy-start(f32[3,96,10]{1,0,2:T(4,128)} %param.11) | copy-start | bytes 34564
  270.2 239.6 %all-to-all-start = ((bf16[64,10,5120]{2,1,0:T(8,128)(2,1)}), bf16[64,10,5120]{2,1,0:T(8,128)(2,1)}, u32[]{:S(2)}, u32[]{:S(2)}) async-start(bf16[64,10,5120]{2,1,0:T(8,128)(2,1)} %bitcast.38), calls=%async_computation | async-start | bytes 20971520 | tf_op jit(solution)/shard_map/all_to_all | solution.py:85
  280.0 44.9 %all-gather.2.cloned.1.call-start = ((), (), s32[]{:S(2)}) async-start(), calls=%async_computation.4 | async-start | bytes 3686400 | tf_op jit(solution)/shard_map/all_gather | solution.py:54
  283.2 320.5 %reduce-scatter.2.cloned.1.call-start = ((), (), s32[]{:S(2)}) async-start(), calls=%async_computation.5 | async-start | bytes 7372800 | tf_op jit(solution)/shard_map/reduce_scatter | solution.py:104
  324.9 6.1 collective-permute-start
  353.5 5.9 copy-start
  522.6 5.9 copy-start.1
  522.6 12.3 %slice-start = ((s8[6553600]{0:T(1024)(128)(4,1)}), s8[2359296]{0:T(1024)(128)(4,1)S(1)}, s32[]{:S(2)}) async-start(s8[6553600]{0:T(1024)(128)(4,1)} %bitcast.41), calls=%async_computation.6 | async-start | bytes 4718592
  528.5 6.3 slice-start.1
  562.2 240.0 %all-to-all-start.2 = ((bf16[64,10,5120]{2,1,0:T(8,128)(2,1)}), bf16[64,10,5120]{2,1,0:T(8,128)(2,1)}, u32[]{:S(2)}, u32[]{:S(2)}) async-start(bf16[64,10,5120]{2,1,0:T(8,128)(2,1)} %all_to_all.28), calls=%async_computation.2 | async-start | bytes 20971520 | tf_op jit(solution)/shard_map/all_to_all | solution.py:114
  572.5 35.7 %copy-start.2 = (bf16[3,96,1280]{2,1,0:T(8,128)(2,1)S(1)}, bf16[3,96,1280]{2,1,0:T(8,128)(2,1)}, u32[]{:S(2)}) copy-start(bf16[3,96,1280]{2,1,0:T(8,128)(2,1)} %param.10) | copy-start | bytes 2211844
  603.7 4.5 copy-start.3
  603.7 4.5 copy-start.4
  605.6 2.6 collective-permute-start.1
Sparse Core Ops, SparseCore 0:
  283.3 41.5 all-gather.1
  539.9 63.7 reduce-scatter.1
where the time goes:
time: 824 us; the launch traced here: 820 us
  waiting for transfers between devices  645 us (78%)
  local copies, waits for them, and re-layouts  58.8 us (7%)
  matrix products  39.3 us (5%)
  starting transfers between devices  34.8 us (4%)
  other arithmetic  28.2 us (3%)
  between operations  14.3 us (2%)
    all_to_all x1, waiting for transfers between devices, shards(): lax.all_to_all(replicate(send_rows), 'dev', split_axis=0, concat_axis=0,...  227 us
    all_to_all x1, waiting for transfers between devices, shards(): lax.all_to_all(partial_term, 'dev', split_axis=0, concat_axis=0, tiled=True)  191 us
    all_to_all x1, waiting for transfers between devices, shards(): lax.all_to_all(replicate(send_cot), 'dev', split_axis=0, concat_axis=0, t...  146 us
    all_gather x1, waiting for transfers between devices, shards(): gathered = lax.all_gather(owned, 'group', axis=2, tiled=True)  41.7 us
    reduce_scatter x1, waiting for transfers between devices, shards(): lax.psum_scatter(jnp.stack([gate_grad, upward_grad, down_grad]).astype(jn...  31.2 us
  transfers between devices with their start and end apart: 7, of which 7 were waited for; matrix products, arithmetic and copies ran while one was open for 5% of the time, Pallas kernels for 0%

commit v1 on v0

v1 whole, which is shorter than its diff:
```python
import jax
import jax.numpy as jnp
from jax import lax
from jax.experimental import pallas as pl
from jax.experimental.pallas import tpu as pltpu
from jax.sharding import PartitionSpec as P

MESH = pl.DeviceIdType.MESH
QB = 128
NZ, NX, NY = 8, 4, 4
CAP = 20
SLAB = 2 * CAP
NEAR = (1, 7, 2, 6, 3, 5, 4)
HBM = pl.BlockSpec(memory_space=pltpu.HBM)

BETA_ONE = 0.9
BETA_TWO = 0.999
LEARNING_RATE = 0.01
ADAM_EPS = 1e-08
STEP_COUNT = 10


def place():
    dev = lax.axis_index("dev")
    return lax.axis_index("group"), dev // 8, (dev // 2) % 4, dev % 2


def device(y, z, x, c):
    return (y, (z * NX + x) * 2 + c)


def along_z(k):
    y, z, x, c = place()
    return device(y, (z + k) % NZ, x, c)


def along_y(k):
    y, z, x, c = place()
    return device((y + k) % NY, z, x, c)


def token_pair():
    y, z, x, c = place()
    return device(y, z, x + 1 - 2 * (x % 2), c)


def weight_pair():
    y, z, x, c = place()
    return device(y, z, 3 - x, c)


def other_core():
    y, z, x, c = place()
    return device(y, z, x, 1 - c)


def greet(peers):
    barrier = pltpu.get_barrier_semaphore()
    for peer in peers:
        pl.semaphore_signal(barrier, inc=1, device_id=peer, device_id_type=MESH)
    pl.semaphore_wait(barrier, len(peers))


def dispatch_kernel(slabs, owned, rows, weights, z_send, z_recv, x_send, x_recv, c_send, c_recv, w_send, w_recv, local):
    y = lax.axis_index("group")
    width = owned.shape[2]
    greet(
        [along_z(k) for k in range(1, NZ)]
        + [along_y(k) for k in range(1, NY)]
        + [token_pair(), weight_pair(), other_core()]
    )

    def remote(src, dst, send, recv, peer):
        copy = pltpu.make_async_remote_copy(
            src, dst, send, recv, device_id=peer, device_id_type=MESH
        )
        copy.start()
        return copy

    mine = pl.ds(pl.multiple_of(y * width, width), width)
    to_z = {}
    for k in NEAR:
        to_z[k] = remote(slabs.at[k], rows.at[0, 0, k], z_send.at[k], z_recv.at[k], along_z(k))
    keep_rows = pltpu.make_async_copy(slabs.at[0], rows.at[0, 0, 0], local.at[0])
    keep_rows.start()
    keep_weights = pltpu.make_async_copy(owned, weights.at[:, 0, :, mine], local.at[1])
    keep_weights.start()
    to_partner = remote(owned, weights.at[:, 1, :, mine], w_send.at[0], w_recv.at[0], weight_pair())
    to_y = [
        remote(owned, weights.at[:, 0, :, mine], w_send.at[k], w_recv.at[k], along_y(k))
        for k in range(1, NY)
    ]

    to_x, to_c = [], []

    def spread(k):
        to_x.append(
            remote(rows.at[0, 0, k], rows.at[0, 1, k], x_send.at[k], x_recv.at[k], token_pair())
        )
        to_c.append(
            remote(rows.at[0, 0, k], rows.at[1, 0, k], c_send.at[0, k], c_recv.at[0, k], other_core())
        )

    def cross(at, k):
        to_x[at].wait_recv()
        to_c.append(
            remote(rows.at[0, 1, k], rows.at[1, 1, k], c_send.at[1, k], c_recv.at[1, k], other_core())
        )

    keep_rows.wait()
    spread(0)
    to_partner.wait_recv()
    for k in range(1, NY):
        to_y.append(
            remote(
                weights.at[:, 1, :, mine],
                weights.at[:, 1, :, mine],
                w_send.at[NY - 1 + k],
                w_recv.at[NY - 1 + k],
                along_y(k),
            )
        )
    order = (0,) + NEAR
    for at in range(1, NZ):
        to_z[order[at]].wait_recv()
        spread(order[at])
        cross(at - 1, order[at - 1])
    cross(NZ - 1, order[NZ - 1])
    keep_weights.wait()
    to_partner.wait_send()
    for copy in to_y + to_c:
        copy.wait()
    for copy in to_x:
        copy.wait_send()
    for k in NEAR:
        to_z[k].wait_send()


def dispatch(slabs, owned):
    _, slab, features = slabs.shape
    dma = pltpu.SemaphoreType.DMA
    return pl.pallas_call(
        dispatch_kernel,
        out_shape=(
            jax.ShapeDtypeStruct((2, 2, NZ, slab, features), jnp.bfloat16),
            jax.ShapeDtypeStruct((3, 2, owned.shape[1], features), jnp.bfloat16),
        ),
        in_specs=[HBM, HBM],
        out_specs=(HBM, HBM),
        scratch_shapes=[
            dma((NZ,)),
            dma((NZ,)),
            dma((NZ,)),
            dma((NZ,)),
            dma((2, NZ)),
            dma((2, NZ)),
            dma((2 * NY - 1,)),
            dma((2 * NY - 1,)),
            dma((2,)),
        ],
        compiler_params=pltpu.CompilerParams(collective_id=0, has_side_effects=True),
        name="dispatch",
    )(slabs, owned)


def exchange(name, number, values, moves, results):
    peers = []
    for move in moves:
        if move[0] not in peers:
            peers.append(move[0])

    def kernel(*refs):
        sources = refs[: len(values)]
        targets = refs[len(values) : len(values) + len(results)]
        send, recv = refs[len(values) + len(results) :]
        greet([peer() for peer in peers])
        copies = []
        for at, (peer, source, source_index, target, target_index) in enumerate(moves):
            src, dst = sources[source], targets[target]
            if source_index is not None:
                src = src.at[source_index()]
            if target_index is not None:
                dst = dst.at[target_index()]
            copy = pltpu.make_async_remote_copy(
                src, dst, send.at[at], recv.at[at], device_id=peer(), device_id_type=MESH
            )
            copy.start()
            copies.append(copy)
        for copy in copies:
            copy.wait()

    return pl.pallas_call(
        kernel,
        out_shape=tuple(results),
        in_specs=[HBM] * len(values),
        out_specs=(HBM,) * len(results),
        scratch_shapes=[
            pltpu.SemaphoreType.DMA((len(moves),)),
            pltpu.SemaphoreType.DMA((len(moves),)),
        ],
        compiler_params=pltpu.CompilerParams(collective_id=number, has_side_effects=True),
        name=name,
    )(*values)


def peers_of(shift, count):
    return [(lambda k=k: shift(k)) for k in range(1, count)]


def shards(tokens, cotangent, routes, codes, scales, first_moment, second_moment):
    row_count, features = tokens.shape
    stored, width = codes.shape[1:]
    y, z, _, _ = place()
    owned_full = codes.astype(jnp.float32) * jnp.repeat(scales, QB, axis=2)
    owned = owned_full.astype(jnp.bfloat16)

    route_ids = routes[:, 0]
    matches = route_ids[:, None] == jnp.arange(NZ, dtype=jnp.int32)[None, :]
    counted = matches.astype(jnp.int32)
    earlier = jnp.cumsum(counted, axis=0) - counted
    position = jnp.sum(jnp.where(matches, earlier, 0), axis=1)
    ahead = (route_ids - z + NZ) % NZ
    row_range = jnp.arange(row_count, dtype=jnp.int32)
    slab_range = jnp.arange(NZ * SLAB, dtype=jnp.int32)
    packing = jnp.concatenate(
        [
            (slab_range[:, None] == (ahead * SLAB + position + half * CAP)[None, :])
            for half in (0, 1)
        ],
        axis=1,
    ).astype(jnp.bfloat16)
    both = jnp.concatenate([tokens, cotangent], axis=0)
    slabs = (
        jnp.dot(packing, both, preferred_element_type=jnp.float32)
        .astype(jnp.bfloat16)
        .reshape(NZ, SLAB, features)
    )

    rows, weights = dispatch(slabs, owned)
    units = 2 * stored
    pieces = 4 * NZ
    flat_rows = rows.reshape(pieces * SLAB, features)
    flat_weights = weights.reshape(3 * units, features)
    pre = lax.dot_general(
        flat_rows, flat_weights, (((1,), (1,)), ((), ())), preferred_element_type=jnp.float32
    ).reshape(pieces, SLAB, 3 * units)
    gate = pre[:, :CAP, :units]
    up = pre[:, :CAP, units : 2 * units]
    hidden_cot = pre[:, CAP:, 2 * units :]
    sig = jax.nn.sigmoid(gate)
    activated = gate * sig
    hidden = (activated * up).astype(jnp.bfloat16)
    gate_cot = (hidden_cot * up * sig * (1.0 + gate * (1.0 - sig))).astype(jnp.bfloat16)
    up_cot = (hidden_cot * activated).astype(jnp.bfloat16)
    cots = jnp.concatenate([gate_cot, up_cot], axis=2)
    blank = jnp.zeros_like(cots)
    mixed = jnp.concatenate(
        [
            jnp.concatenate([cots, jnp.zeros_like(hidden)], axis=2),
            jnp.concatenate([blank, hidden], axis=2),
        ],
        axis=1,
    ).reshape(pieces * SLAB, 3 * units)
    grads = (
        lax.dot_general(
            mixed, flat_rows, (((0,), (0,)), ((), ())), preferred_element_type=jnp.float32
        )
        .astype(jnp.bfloat16)
        .reshape(3, 2, stored, features)
    )
    half_width = features // 2
    spread = jnp.concatenate(
        [
            jnp.concatenate([cots, blank], axis=2),
            jnp.concatenate([blank, cots], axis=2),
        ],
        axis=1,
    ).reshape(pieces * SLAB, 4 * units)
    in_weights = flat_weights[: 2 * units]
    stacked = jnp.concatenate([in_weights[:, :half_width], in_weights[:, half_width:]], axis=0)
    terms = (
        jnp.dot(spread, stacked, preferred_element_type=jnp.float32)
        .astype(jnp.bfloat16)
        .reshape(2, 2, NZ, SLAB, half_width)
    )

    def total(first, *others):
        result = first.astype(jnp.float32)
        for other in others:
            result = result + other.astype(jnp.float32)
        return result

    slab_set = jax.ShapeDtypeStruct((2, NZ, SLAB, half_width), jnp.bfloat16)
    (crossed,) = exchange(
        "cores", 1, (terms,), [(other_core, 0, lambda: 1, 0, None)], [slab_set]
    )
    chip_terms = total(terms[0], crossed).astype(jnp.bfloat16)

    def columns(k):
        start = (lax.axis_index("group") + k) % NY * width
        return pl.ds(pl.multiple_of(start, width), width)

    def shares(matrices, number):
        return [
            (
                (lambda k=k: along_y(k)),
                number,
                (lambda k=k: (matrices, slice(None), slice(None), columns(k))),
                number,
                (lambda k=k: k - 1),
            )
            for k in range(1, NY)
        ]

    paired, first_shares = exchange(
        "pairs",
        2,
        (chip_terms, grads),
        [(token_pair, 0, lambda: 1, 0, None)] + shares(pl.ds(0, 2), 1),
        [
            jax.ShapeDtypeStruct((NZ, SLAB, half_width), jnp.bfloat16),
            jax.ShapeDtypeStruct((NY - 1, 2, 2, stored, width), jnp.bfloat16),
        ],
    )
    slot_grads = total(chip_terms[0], paired).astype(jnp.bfloat16)
    back = [
        ((lambda k=k: along_z(NZ - k)), 0, (lambda k=k: k), 0, (lambda k=k: k)) for k in NEAR
    ]
    returned, last_shares = exchange(
        "returns",
        3,
        (slot_grads, grads),
        back + shares(pl.ds(2, 1), 1),
        [
            jax.ShapeDtypeStruct((NZ, SLAB, half_width), jnp.bfloat16),
            jax.ShapeDtypeStruct((NY - 1, 1, 2, stored, width), jnp.bfloat16),
        ],
    )
    own_shares = lax.dynamic_slice_in_dim(grads, y * width, width, axis=3)
    summed = jnp.concatenate(
        [total(own_shares[:2], *first_shares), total(own_shares[2:], *last_shares)], axis=0
    )
    (given,) = exchange(
        "blocks",
        4,
        (summed[:, 1].astype(jnp.bfloat16),),
        [(weight_pair, 0, None, 0, None)],
        [jax.ShapeDtypeStruct((3, stored, width), jnp.bfloat16)],
    )
    gradient = summed[:, 0] + given.astype(jnp.float32)

    returned = jnp.concatenate([slot_grads[:1], returned[1:]], axis=0)
    flat_returned = returned.reshape(NZ * SLAB, half_width)
    grad_tokens = jnp.concatenate(
        [
            jnp.dot(
                ((ahead * SLAB + position + half * CAP)[:, None] == slab_range[None, :]).astype(
                    jnp.bfloat16
                ),
                flat_returned,
                preferred_element_type=jnp.float32,
            ).astype(jnp.bfloat16)
            for half in (0, 1)
        ],
        axis=1,
    )
    new_first = BETA_ONE * first_moment + (1.0 - BETA_ONE) * gradient
    new_second = BETA_TWO * second_moment + (1.0 - BETA_TWO) * gradient * gradient
    first_fix = 1.0 - BETA_ONE**STEP_COUNT
    second_fix = 1.0 - BETA_TWO**STEP_COUNT
    new_weights = owned_full - LEARNING_RATE * (new_first / first_fix) / (
        jnp.sqrt(new_second / second_fix) + ADAM_EPS
    )
    return (grad_tokens, new_weights, new_first, new_second)


def solution(mesh):
    stored = P(None, "dev", "group")
    spread = P(("group", "dev"), None)
    return jax.shard_map(
        shards,
        mesh=mesh,
        in_specs=(spread, spread, spread, stored, stored, stored, stored),
        out_specs=(spread, stored, stored, stored),
        check_vma=False,
    )
```

time: 824 us -> 280 us (0.34)
  waiting for transfers between devices: 645 us -> 0 us
  Pallas kernels: 0 us -> 205 us
  local copies, waits for them, and re-layouts: 58.8 us -> 8.03 us
  starting transfers between devices: 34.8 us -> 0 us
  between operations: 14.3 us -> 0.98 us
    all_to_all x3 -> x0, waiting for transfers between devices: 565 us -> none  [the longest x1 227 us: shards(): lax.all_to_all(replicate(send_rows), 'dev', split_axis=0, concat_axis=0,...]
    pallas_call x0 -> x5, Pallas kernels: none -> 205 us  [the longest x4 108 us: exchange(): pl.pallas_call(kernel, out_shape=tuple(results), in_specs=[HBM] * len(val...]
    all_gather x1 -> x0, waiting for transfers between devices: 41.7 us -> none  [shards(): gathered = lax.all_gather(owned, 'group', axis=2, tiled=True)]
    all_to_all x3 -> x0, local copies, waits for them, and re-layouts: 38.5 us -> none  [the longest x1 12.9 us: shards(): lax.all_to_all(replicate(send_cot), 'dev', split_axis=0, concat_axis=0, t...]
    all_to_all x3 -> x0, starting transfers between devices: 33.3 us -> none  [the longest x1 13.2 us: shards(): lax.all_to_all(replicate(send_rows), 'dev', split_axis=0, concat_axis=0,...]
    reduce_scatter x1 -> x0, waiting for transfers between devices: 31.2 us -> none  [shards(): lax.psum_scatter(jnp.stack([gate_grad, upward_grad, down_grad]).astype(jn...]
    broadcast_in_dim x4 -> x2, local copies, waits for them, and re-layouts: 15.4 us -> 0.06 us  [the longest x1 0.05 us: shards(): blank = jnp.zeros_like(cots)]
    select_n x1 -> x0, other arithmetic: 9.64 us -> none  [shards(): jnp.where(lower_copy, jnp.concatenate([gathered, partner], axis=1), jnp.c...]
  transfers between devices with their start and end apart: 7 -> 0, of which waited for: 7 -> 0; matrix products, arithmetic and copies ran while one was open for 5% -> 0% of each run, Pallas kernels for 0% -> 0%
where the time goes in v1:
time: 280 us; the launch traced here: 276 us
  Pallas kernels  205 us (73%)
  matrix products  36.1 us (13%)
  other arithmetic  26.5 us (9%)
  local copies, waits for them, and re-layouts  8.03 us (3%)
    pallas_call x4, Pallas kernels, exchange(): pl.pallas_call(kernel, out_shape=tuple(results), in_specs=[HBM] * len(val...  108 us
    pallas_call x1, Pallas kernels, dispatch(): pl.pallas_call(dispatch_kernel, out_shape=(jax.ShapeDtypeStruct((2, 2, NZ...  97 us
    dot_general x1, matrix products, shards(): lax.dot_general(flat_rows, flat_weights, (((1,), (1,)), ((), ())), prefer...  14.9 us
    dot_general x1, matrix products, shards(): lax.dot_general(mixed, flat_rows, (((0,), (0,)), ((), ())), preferred_ele...  9.98 us
    dot_general x1, matrix products, shards(): jnp.dot(spread, stacked, preferred_element_type=jnp.float32)  5.71 us

profile of v1, /device:TPU:1, one launch (start us, length us, event | category | flops | bytes accessed | tf_op | source)
XLA Modules:
  0.0 276.2 jit_solution(9524728192423801369)
XLA Ops:
  0.6 0.7 fusion.23
  1.4 0.2 reduce_window_sum.11
  1.6 0.8 select_reduce_fusion
  2.4 0.7 broadcast_add_fusion
  3.1 0.1 iota_compare_fusion.5
  3.1 0.0 copy-start.5
  3.1 4.5 %convolution_convert_fusion.2 = bf16[320,5120]{1,0:T(8,128)(2,1)} fusion(bf16[128,5120]{1,0:T(8,128)(2,1)} %param.8, bf16[128,5120]{1,0:T(8,128)(2,1)} %param.7, pred[320,128]{1,0:T(32,128)(4,1)S(1)} %get-tuple-element.28, pred[320,128]{1,0:T(32,128)(4,1)S(1)} %get-tuple-element.29), kind=kOutput, calls=%fused_computation.2 | convolution fusion | flops 845824000 | bytes 5980160 | tf_op jit(solution)/shard_map/dot_general | solution.py:234
  7.6 0.1 broadcast_in_dim.11
  7.8 0.8 copy.18
  8.6 2.1 fusion.15.owned
  10.7 97.0 %dispatch.1 = (bf16[2,2,8,40,5120]{4,3,2,1,0:T(8,128)(2,1)}, bf16[3,2,96,5120]{3,2,1,0:T(8,128)(2,1)}) custom-call(bf16[8,40,5120]{2,1,0:T(8,128)(2,1)} %bitcast.86, bf16[3,96,1280]{2,1,0:T(8,128)(2,1)} %fusion.15.owned), custom_call_target="tpu_custom_call" | custom-call | tf_op jit(solution)/shard_map/dispatch/pallas_call | solution.py:142
  107.7 0.0 slice-start.3
  107.7 0.0 slice-start.4
  107.7 0.0 slice-start.6
  107.7 14.9 %fusion.37 = f32[32,40,576]{2,1,0:T(8,128)S(1)} fusion(bf16[32,40,5120]{2,1,0:T(8,128)(2,1)} %bitcast.95, bf16[576,5120,1]{1,0,2:T(8,128)(2,1)} %bitcast.87), kind=kOutput, calls=%fused_computation.82 | convolution fusion | flops 7549747200 | bytes 21954560 | tf_op jit(solution)/shard_map/dot_general | solution.py:244
  122.6 0.6 multiply_convert_fusion
  123.2 0.0 slice-start.1
  123.2 0.5 fusion.9
  123.7 0.0 slice-start.2
  123.8 10.0 %convolution_convert_fusion.1 = bf16[576,5120]{1,0:T(8,128)(2,1)} fusion(bf16[1280,576]{1,0:T(8,128)(2,1)S(1)} %bitcast.91, bf16[1280,5120]{1,0:T(8,128)(2,1)S(1)} %bitcast.98), kind=kOutput, calls=%fused_computation.1 | convolution fusion | flops 7552696320 | bytes 20480000 | tf_op jit(solution)/shard_map/dot_general | solution.py:265
  133.7 0.3 slice.50
  134.0 0.3 fusion.36
  134.3 0.1 broadcast_in_dim.12
  134.4 1.5 maximum_maximum_fusion
  135.9 5.7 %convolution_convert_fusion = bf16[1280,2560]{1,0:T(8,128)(2,1)S(1)} fusion(bf16[1280,768]{1,0:T(8,128)(2,1)S(1)} %bitcast.90, bf16[384,2560]{1,0:T(8,128)(2,1)S(1)} %get-tuple-element.24, bf16[384,2560]{1,0:T(8,128)(2,1)S(1)} %get-tuple-element.23), kind=kOutput, calls=%fused_computation | convolution fusion | flops 5044305920 | bytes 12451840 | tf_op jit(solution)/shard_map/dot_general | solution.py:282
  141.6 2.1 slice.67
  143.7 1.6 copy-done.1
  145.3 6.2 %cores.1 = bf16[2,8,40,2560]{3,2,1,0:T(8,128)(2,1)} custom-call(bf16[2,2,8,40,2560]{4,3,2,1,0:T(8,128)(2,1)} %bitcast.81), custom_call_target="tpu_custom_call" | custom-call | tf_op jit(solution)/shard_map/cores/pallas_call | solution.py:192
  151.5 5.5 %fusion.refs_0_ = bf16[2,8,40,2560]{3,2,1,0:T(8,128)(2,1)} fusion(bf16[2,8,40,2560]{3,2,1,0:T(8,128)(2,1)} %bitcast.84, bf16[2,8,40,2560]{3,2,1,0:T(8,128)(2,1)} %cores.1), kind=kLoop, calls=%fused_computation.4 | loop fusion | flops 6553600 | bytes 9830400 | tf_op jit(solution)/shard_map/convert_element_type | solution.py:297
  156.9 47.1 %pairs.1 = (bf16[8,40,2560]{2,1,0:T(8,128)(2,1)}, bf16[3,2,2,96,1280]{4,3,2,1,0:T(8,128)(2,1)}) custom-call(bf16[2,8,40,2560]{3,2,1,0:T(8,128)(2,1)} %fusion.refs_0_, bf16[3,2,96,5120]{3,2,1,0:T(8,128)(2,1)} %bitcast.76), custom_call_target="tpu_custom_call" | custom-call | tf_op jit(solution)/shard_map/pairs/pallas_call | solution.py:192
  204.1 2.7 convert_add_fusion.2
  206.8 0.4 copy-done
  207.2 0.5 copy-done.3
  207.7 1.6 fusion.4.refs_0_
  209.3 37.7 %returns.1 = (bf16[8,40,2560]{2,1,0:T(8,128)(2,1)}, bf16[3,1,2,96,1280]{4,3,2,1,0:T(8,128)(2,1)}) custom-call(bf16[8,40,2560]{2,1,0:T(8,128)(2,1)} %fusion.4.refs_0_, bf16[3,2,96,5120]{3,2,1,0:T(8,128)(2,1)} %bitcast.78), custom_call_target="tpu_custom_call" | custom-call | tf_op jit(solution)/shard_map/returns/pallas_call | solution.py:192
  247.0 1.7 convert_add_fusion.5
  248.7 0.0 copy-start.2
  248.7 0.9 copy-done.2
  249.7 0.9 fusion.17.refs_0_
  250.6 16.6 %blocks.1 = bf16[3,96,1280]{2,1,0:T(8,128)(2,1)} custom-call(bf16[3,96,1280]{2,1,0:T(8,128)(2,1)} %fusion.17.refs_0_), custom_call_target="tpu_custom_call" | custom-call | tf_op jit(solution)/shard_map/blocks/pallas_call | solution.py:192
  267.2 5.6 %divide_subtract_fusion = (f32[3,96,1280]{2,1,0:T(8,128)}, f32[3,96,1280]{2,1,0:T(8,128)}, f32[3,96,1280]{2,1,0:T(8,128)}) fusion(f32[3,96,1280]{2,1,0:T(8,128)S(1)} %copy.18, bf16[3,96,1280]{2,1,0:T(8,128)(2,1)} %param.10, bf16[3,96,1280]{2,1,0:T(8,128)(2,1)} %blocks.1, f32[1,2,96,1280]{3,2,0,1:T(8,128)} %copy-done.2, ...), kind=kLoop, calls=%fused_computation.33 | loop fusion | flops 7004160 | bytes 13271040 | tf_op jit(solution)/shard_map/sub | solution.py:371
  272.8 0.1 slice.57
  272.9 0.0 copy-start.6
  272.9 0.8 slice-done
  273.7 0.1 pad_maximum_fusion
  273.9 0.5 convolution_convert_fusion.4
  274.5 0.5 convolution_convert_fusion.3
  275.0 1.2 pad_maximum_fusion.2
  (21 shorter events, 0.1 us)
Async XLA Ops:
  3.1 4.5 %copy-start.5 = (f32[3,96,10]{1,0,2:T(4,128)S(1)}, f32[3,96,10]{1,0,2:T(4,128)}, u32[]{:S(2)}) copy-start(f32[3,96,10]{1,0,2:T(4,128)} %param.11) | copy-start | bytes 34564
  107.7 16.0 %slice-start.3 = ((s8[13107200]{0:T(1024)(128)(4,1)}), s8[4194304]{0:T(1024)(128)(4,1)S(1)}, s32[]{:S(2)}) async-start(s8[13107200]{0:T(1024)(128)(4,1)} %bitcast.96), calls=%async_computation.3 | async-start | bytes 8388608
  107.7 16.0 %slice-start.4 = ((s8[13107200]{0:T(1024)(128)(4,1)}), s8[4194304]{0:T(1024)(128)(4,1)S(1)}, s32[]{:S(2)}) async-start(s8[13107200]{0:T(1024)(128)(4,1)} %bitcast.96), calls=%async_computation.4 | async-start | bytes 8388608
  107.7 16.0 %slice-start.5 = ((s8[13107200]{0:T(1024)(128)(4,1)}), s8[4194304]{0:T(1024)(128)(4,1)S(1)}, s32[]{:S(2)}) async-start(s8[13107200]{0:T(1024)(128)(4,1)} %bitcast.96), calls=%async_computation.5 | async-start | bytes 8388608
  107.7 16.0 %slice-start.6 = ((s8[13107200]{0:T(1024)(128)(4,1)}), s8[524288]{0:T(1024)(128)(4,1)S(1)}, s32[]{:S(2)}) async-start(s8[13107200]{0:T(1024)(128)(4,1)} %bitcast.96), calls=%async_computation.6 | async-start | bytes 1048576
  123.2 10.6 %slice-start.1 = ((s8[5898240]{0:T(1024)(128)(4,1)}), s8[4194304]{0:T(1024)(128)(4,1)S(1)}, s32[]{:S(2)}) async-start(s8[5898240]{0:T(1024)(128)(4,1)} %bitcast.88), calls=%async_computation.1 | async-start | bytes 8388608
  123.7 10.0 %slice-start.2 = ((s8[5898240]{0:T(1024)(128)(4,1)}), s8[1703936]{0:T(1024)(128)(4,1)S(1)}, s32[]{:S(2)}) async-start(s8[5898240]{0:T(1024)(128)(4,1)} %bitcast.88), calls=%async_computation.2 | async-start | bytes 3407872
  141.6 3.7 %copy-start.1 = (bf16[1280,2560]{1,0:T(8,128)(2,1)}, bf16[1280,2560]{1,0:T(8,128)(2,1)S(1)}, u32[]{:S(2)}) copy-start(bf16[1280,2560]{1,0:T(8,128)(2,1)S(1)} %convolution_convert_fusion) | copy-start | bytes 19660804
  204.1 3.1 %copy-start = (bf16[2,8,40,2560]{3,2,1,0:T(8,128)(2,1)S(1)}, bf16[2,8,40,2560]{3,2,1,0:T(8,128)(2,1)}, u32[]{:S(2)}) copy-start(bf16[2,8,40,2560]{3,2,1,0:T(8,128)(2,1)} %fusion.refs_0_) | copy-start | bytes 9830404
  204.1 3.6 %copy-start.3 = (bf16[8,40,2560]{2,1,0:T(8,128)(2,1)S(1)}, bf16[8,40,2560]{2,1,0:T(8,128)(2,1)}, u32[]{:S(2)}) copy-start(bf16[8,40,2560]{2,1,0:T(8,128)(2,1)} %get-tuple-element.12) | copy-start | bytes 4915204
  248.7 0.9 copy-start.2
  267.2 5.6 %copy-start.4 = (bf16[8,40,2560]{2,1,0:T(8,128)(2,1)S(1)}, bf16[8,40,2560]{2,1,0:T(8,128)(2,1)}, u32[]{:S(2)}) copy-start(bf16[8,40,2560]{2,1,0:T(8,128)(2,1)} %get-tuple-element.13) | copy-start | bytes 4915204
  272.8 0.9 slice-start
  272.9 1.0 copy-start.6

commit v2 on v1

--- a/solution.py
+++ b/solution.py
@@ -163,48 +163,163 @@
     )(slabs, owned)
 
 
-def exchange(name, number, values, moves, results):
-    peers = []
-    for move in moves:
-        if move[0] not in peers:
-            peers.append(move[0])
-
-    def kernel(*refs):
-        sources = refs[: len(values)]
-        targets = refs[len(values) : len(values) + len(results)]
-        send, recv = refs[len(values) + len(results) :]
-        greet([peer() for peer in peers])
-        copies = []
-        for at, (peer, source, source_index, target, target_index) in enumerate(moves):
-            src, dst = sources[source], targets[target]
-            if source_index is not None:
-                src = src.at[source_index()]
-            if target_index is not None:
-                dst = dst.at[target_index()]
-            copy = pltpu.make_async_remote_copy(
-                src, dst, send.at[at], recv.at[at], device_id=peer(), device_id_type=MESH
+FAR = (4, 3, 5, 2, 6, 1, 7, 0)
+
+
+def combine_kernel(
+    terms, grads, returned, gradient,
+    crossed, chip, paired, slot, from_x, block, from_y, from_y_block, given, part,
+    c_send, c_recv, x_send, x_recv, z_send, z_recv, g_send, g_recv, y_send, y_recv, b_send, b_recv, t_send, t_recv, local,
+):
+    f32, bf16 = jnp.float32, jnp.bfloat16
+    y = lax.axis_index("group")
+    width = gradient.shape[2]
+    half = gradient.shape[1] // 2
+    low, high = pl.ds(0, half), pl.ds(half, half)
+
+    def columns(k):
+        return pl.ds(pl.multiple_of((y + k) % NY * width, width), width)
+
+    def remote(src, dst, send, recv, peer):
+        copy = pltpu.make_async_remote_copy(
+            src, dst, send, recv, device_id=peer, device_id_type=MESH
+        )
+        copy.start()
+        return copy
+
+    greet(
+        [along_z(k) for k in range(1, NZ)]
+        + [along_y(k) for k in range(1, NY)]
+        + [token_pair(), weight_pair(), other_core()]
+    )
+    to_c = {
+        k: remote(terms.at[1, :, k], crossed.at[k], c_send.at[k], c_recv.at[k], other_core())
+        for k in FAR
+    }
+    to_g = [
+        remote(grads.at[m, 1, high], from_x.at[m], g_send.at[m], g_recv.at[m], weight_pair())
+        for m in range(3)
+    ]
+    to_y = [
+        remote(
+            grads.at[:, :, low, columns(k)], from_y.at[k - 1], y_send.at[k], y_recv.at[k], along_y(k)
+        )
+        for k in range(1, NY)
+    ]
+    to_x, to_z, to_b, to_t = {}, {}, [], []
+    for k in FAR:
+        to_c[k].wait_recv()
+        chip[1, k] = (terms[0, 1, k].astype(f32) + crossed[k, 1].astype(f32)).astype(bf16)
+        to_x[k] = remote(chip.at[1, k], paired.at[k], x_send.at[k], x_recv.at[k], token_pair())
+        chip[0, k] = (terms[0, 0, k].astype(f32) + crossed[k, 0].astype(f32)).astype(bf16)
+
+    def back(k):
+        to_x[k].wait_recv()
+        slot[k] = (chip[0, k].astype(f32) + paired[k].astype(f32)).astype(bf16)
+        if k:
+            to_z[k] = remote(
+                slot.at[k], returned.at[k], z_send.at[k], z_recv.at[k], along_z(NZ - k)
             )
-            copy.start()
-            copies.append(copy)
-        for copy in copies:
-            copy.wait()
-
+
+    def through(m):
+        to_g[m].wait_recv()
+        block[m] = (grads[m, 0, high].astype(f32) + from_x[m].astype(f32)).astype(bf16)
+        for k in range(1, NY):
+            to_b.append(
+                remote(
+                    block.at[m, :, columns(k)],
+                    from_y_block.at[k - 1, m],
+                    b_send.at[m, k],
+                    b_recv.at[m, k],
+                    along_y(k),
+                )
+            )
+
+    mine = columns(0)
+    back(FAR[0])
+    back(FAR[1])
+    through(0)
+    back(FAR[2])
+    back(FAR[3])
+    through(1)
+    back(FAR[4])
+    back(FAR[5])
+    back(FAR[6])
+    through(2)
+    for copy in to_y:
+        copy.wait_recv()
+    for m in range(3):
+        for b in (1, 0):
+            total = grads[m, b, low, mine].astype(f32)
+            for k in range(NY - 1):
+                total = total + from_y[k, m, b].astype(f32)
+            if b:
+                part[m] = total.astype(bf16)
+                to_t.append(
+                    remote(part.at[m], given.at[m], t_send.at[m], t_recv.at[m], weight_pair())
+                )
+            else:
+                gradient[m, low] = total
+    back(FAR[7])
+    keep = pltpu.make_async_copy(slot.at[0], returned.at[0], local)
+    keep.start()
+    for copy in to_b:
+        copy.wait_recv()
+    for m in range(3):
+        total = block[m, :, mine].astype(f32)
+        for k in range(NY - 1):
+            total = total + from_y_block[k, m].astype(f32)
+        gradient[m, high] = total
+        to_t[m].wait_recv()
+        gradient[m, low] = gradient[m, low] + given[m].astype(f32)
+    keep.wait()
+    for k in FAR:
+        to_c[k].wait_send()
+        to_x[k].wait_send()
+        if k:
+            to_z[k].wait()
+    for copy in to_g + to_y + to_b + to_t:
+        copy.wait_send()
+
+
+def combine(terms, grads):
+    _, _, _, slab, half_width = terms.shape
+    _, _, stored, features = grads.shape
+    width, half = features // NY, stored // 2
+    dma = pltpu.SemaphoreType.DMA
+    bf16 = jnp.bfloat16
+    vmem = pl.BlockSpec(memory_space=pltpu.VMEM)
     return pl.pallas_call(
-        kernel,
-        out_shape=tuple(results),
-        in_specs=[HBM] * len(values),
-        out_specs=(HBM,) * len(results),
+        combine_kernel,
+        out_shape=(
+            jax.ShapeDtypeStruct((NZ, slab, half_width), bf16),
+            jax.ShapeDtypeStruct((3, stored, width), jnp.float32),
+        ),
+        in_specs=[vmem, vmem],
+        out_specs=(HBM, vmem),
         scratch_shapes=[
-            pltpu.SemaphoreType.DMA((len(moves),)),
-            pltpu.SemaphoreType.DMA((len(moves),)),
-        ],
-        compiler_params=pltpu.CompilerParams(collective_id=number, has_side_effects=True),
-        name=name,
-    )(*values)
-
-
-def peers_of(shift, count):
-    return [(lambda k=k: shift(k)) for k in range(1, count)]
+            pltpu.VMEM((NZ, 2, slab, half_width), bf16),
+            pltpu.VMEM((2, NZ, slab, half_width), bf16),
+            pltpu.VMEM((NZ, slab, half_width), bf16),
+            pltpu.VMEM((NZ, slab, half_width), bf16),
+            pltpu.VMEM((3, half, features), bf16),
+            pltpu.VMEM((3, half, features), bf16),
+            pltpu.VMEM((NY - 1, 3, 2, half, width), bf16),
+            pltpu.VMEM((NY - 1, 3, half, width), bf16),
+            pltpu.VMEM((3, half, width), bf16),
+            pltpu.VMEM((3, half, width), bf16),
+        ]
+        + [dma((NZ,))] * 6
+        + [dma((3,))] * 2
+        + [dma((NY,))] * 2
+        + [dma((3, NY))] * 2
+        + [dma((3,))] * 2
+        + [dma],
+        compiler_params=pltpu.CompilerParams(
+            collective_id=1, has_side_effects=True, vmem_limit_bytes=48 << 20
+        ),
+        name="combine",
+    )(terms, grads)
 
 
 def shards(tokens, cotangent, routes, codes, scales, first_moment, second_moment):
@@ -284,72 +399,7 @@
         .reshape(2, 2, NZ, SLAB, half_width)
     )
 
-    def total(first, *others):
-        result = first.astype(jnp.float32)
-        for other in others:
-            result = result + other.astype(jnp.float32)
-        return result
-
-    slab_set = jax.ShapeDtypeStruct((2, NZ, SLAB, half_width), jnp.bfloat16)
-    (crossed,) = exchange(
-        "cores", 1, (terms,), [(other_core, 0, lambda: 1, 0, None)], [slab_set]
-    )
-    chip_terms = total(terms[0], crossed).astype(jnp.bfloat16)
-
-    def columns(k):
-        start = (lax.axis_index("group") + k) % NY * width
-        return pl.ds(pl.multiple_of(start, width), width)
-
-    def shares(matrices, number):
-        return [
-            (
-                (lambda k=k: along_y(k)),
-                number,
-                (lambda k=k: (matrices, slice(None), slice(None), columns(k))),
-                number,
-                (lambda k=k: k - 1),
-            )
-            for k in range(1, NY)
-        ]
-
-    paired, first_shares = exchange(
-        "pairs",
-        2,
-        (chip_terms, grads),
-        [(token_pair, 0, lambda: 1, 0, None)] + shares(pl.ds(0, 2), 1),
-        [
-            jax.ShapeDtypeStruct((NZ, SLAB, half_width), jnp.bfloat16),
-            jax.ShapeDtypeStruct((NY - 1, 2, 2, stored, width), jnp.bfloat16),
-        ],
-    )
-    slot_grads = total(chip_terms[0], paired).astype(jnp.bfloat16)
-    back = [
-        ((lambda k=k: along_z(NZ - k)), 0, (lambda k=k: k), 0, (lambda k=k: k)) for k in NEAR
-    ]
-    returned, last_shares = exchange(
-        "returns",
-        3,
-        (slot_grads, grads),
-        back + shares(pl.ds(2, 1), 1),
-        [
-            jax.ShapeDtypeStruct((NZ, SLAB, half_width), jnp.bfloat16),
-            jax.ShapeDtypeStruct((NY - 1, 1, 2, stored, width), jnp.bfloat16),
-        ],
-    )
-    own_shares = lax.dynamic_slice_in_dim(grads, y * width, width, axis=3)
-    summed = jnp.concatenate(
-        [total(own_shares[:2], *first_shares), total(own_shares[2:], *last_shares)], axis=0
-    )
-    (given,) = exchange(
-        "blocks",
-        4,
-        (summed[:, 1].astype(jnp.bfloat16),),
-        [(weight_pair, 0, None, 0, None)],
-        [jax.ShapeDtypeStruct((3, stored, width), jnp.bfloat16)],
-    )
-    gradient = summed[:, 0] + given.astype(jnp.float32)
-
-    returned = jnp.concatenate([slot_grads[:1], returned[1:]], axis=0)
+    returned, gradient = combine(terms, grads)
     flat_returned = returned.reshape(NZ * SLAB, half_width)
     grad_tokens = jnp.concatenate(
         [

time: 280 us -> 209 us (0.75); the launches traced: 276 us -> 209 us
  Pallas kernels: 205 us -> 156 us
  other arithmetic: 26.5 us -> 11.2 us
  local copies, waits for them, and re-layouts: 8.03 us -> 2.87 us
    pallas_call x4 -> x1, Pallas kernels: 108 us -> 58.7 us  [combine(): pl.pallas_call(combine_kernel, out_shape=(jax.ShapeDtypeStruct((NZ, slab,...]
    convert_element_type x3 -> x0, other arithmetic: 7.99 us -> none  [the longest x1 5.46 us: shards(): chip_terms = total(terms[0], crossed).astype(jnp.bfloat16)]
    add x2 -> x0, other arithmetic: 4.41 us -> none  [total(): result = result + other.astype(jnp.float32)]
    slice x4 -> x0, local copies, waits for them, and re-layouts: 3 us -> none  [the longest x1 2.09 us: shards(): chip_terms = total(terms[0], crossed).astype(jnp.bfloat16)]
    sub x1, other arithmetic: 5.6 us -> 2.78 us  [shards(): owned_full - LEARNING_RATE * (new_first / first_fix) / (jnp.sqrt(new_seco...]
where the time goes in v2:
time: 209 us
  Pallas kernels  156 us (75%)
  matrix products  38.1 us (18%)
  other arithmetic  11.2 us (5%)
  local copies, waits for them, and re-layouts  2.87 us (1%)
    pallas_call x1, Pallas kernels, dispatch(): pl.pallas_call(dispatch_kernel, out_shape=(jax.ShapeDtypeStruct((2, 2, NZ...  96.9 us
    pallas_call x1, Pallas kernels, combine(): pl.pallas_call(combine_kernel, out_shape=(jax.ShapeDtypeStruct((NZ, slab,...  58.7 us
    dot_general x1, matrix products, shards(): lax.dot_general(flat_rows, flat_weights, (((1,), (1,)), ((), ())), prefer...  14.9 us
    dot_general x1, matrix products, shards(): lax.dot_general(mixed, flat_rows, (((0,), (0,)), ((), ())), preferred_ele...  10.2 us
    dot_general x1, matrix products, shards(): jnp.dot(spread, stacked, preferred_element_type=jnp.float32)  7.36 us
    dot_general x1, matrix products, shards(): jnp.dot(packing, both, preferred_element_type=jnp.float32)  4.49 us

profile of v2, /device:TPU:1, one launch (start us, length us, event | category | flops | bytes accessed | tf_op | source)
XLA Modules:
  0.0 208.6 jit_solution(15428068223359515446)
XLA Ops:
  0.6 0.7 fusion.16
  1.4 0.2 reduce_window_sum.11
  1.5 0.8 select_reduce_fusion
  2.4 0.7 broadcast_add_fusion
  3.1 0.1 iota_compare_fusion.5
  3.1 0.0 copy-start.4
  3.1 4.5 %convolution_convert_fusion.2 = bf16[320,5120]{1,0:T(8,128)(2,1)} fusion(bf16[128,5120]{1,0:T(8,128)(2,1)} %param.8, bf16[128,5120]{1,0:T(8,128)(2,1)} %param.7, pred[320,128]{1,0:T(32,128)(4,1)S(1)} %get-tuple-element.24, pred[320,128]{1,0:T(32,128)(4,1)S(1)} %get-tuple-element.25), kind=kOutput, calls=%fused_computation.2 | convolution fusion | flops 845824000 | bytes 5980160 | tf_op jit(solution)/shard_map/dot_general | solution.py:349
  7.6 0.0 copy-done.4
  7.6 0.1 broadcast_in_dim.11
  7.8 0.8 copy.13
  8.6 2.2 %fusion.9.owned = bf16[3,96,1280]{2,1,0:T(8,128)(2,1)} fusion(f32[3,96,1280]{2,1,0:T(8,128)S(1)} %copy.13, bf16[3,96,1280]{2,1,0:T(8,128)(2,1)} %param.10), kind=kLoop, calls=%fused_computation.21 | loop fusion | flops 1105920 | bytes 2949120 | tf_op jit(solution)/shard_map/convert_element_type | solution.py:330
  10.7 96.9 %dispatch.1 = (bf16[2,2,8,40,5120]{4,3,2,1,0:T(8,128)(2,1)}, bf16[3,2,96,5120]{3,2,1,0:T(8,128)(2,1)}) custom-call(bf16[8,40,5120]{2,1,0:T(8,128)(2,1)} %bitcast.35, bf16[3,96,1280]{2,1,0:T(8,128)(2,1)} %fusion.9.owned), custom_call_target="tpu_custom_call" | custom-call | tf_op jit(solution)/shard_map/dispatch/pallas_call | solution.py:142
  107.7 14.9 %fusion.30 = f32[32,40,576]{2,1,0:T(8,128)S(1)} fusion(bf16[32,40,5120]{2,1,0:T(8,128)(2,1)} %bitcast.42, bf16[576,5120,1]{1,0,2:T(8,128)(2,1)} %bitcast.36), kind=kOutput, calls=%fused_computation.57 | convolution fusion | flops 7549747200 | bytes 21954560 | tf_op jit(solution)/shard_map/dot_general | solution.py:359
  122.6 0.0 copy-start.1
  122.6 0.6 multiply_convert_fusion
  123.2 0.1 broadcast_in_dim.12
  123.3 1.5 maximum_maximum_fusion
  124.8 0.5 copy-done.1
  125.3 0.3 slice.24
  125.5 0.3 fusion.29
  125.8 0.0 slice-start
  125.8 0.0 slice-start.1
  125.8 0.0 slice-start.2
  125.9 0.0 slice-start.3
  125.9 7.4 %convolution_convert_fusion = bf16[1280,2560]{1,0:T(8,128)(2,1)} fusion(bf16[1280,768]{1,0:T(8,128)(2,1)S(1)} %bitcast.37, bf16[384,2560]{1,0:T(8,128)(2,1)S(1)} %get-tuple-element.20, bf16[384,2560]{1,0:T(8,128)(2,1)S(1)} %get-tuple-element.19), kind=kOutput, calls=%fused_computation | convolution fusion | flops 5044305920 | bytes 12451840 | tf_op jit(solution)/shard_map/dot_general | solution.py:397
  133.2 0.5 fusion.7
  133.7 0.0 slice-done
  133.8 0.0 slice-done.1
  133.8 0.0 slice-done.2
  133.8 0.0 slice-done.3
  133.8 10.2 %convolution_convert_fusion.1 = bf16[576,5120]{1,0:T(8,128)(2,1)} fusion(bf16[1280,576]{1,0:T(8,128)(2,1)S(1)} %bitcast.38, bf16[1280,5120]{1,0:T(8,128)(2,1)S(1)} %bitcast.45), kind=kOutput, calls=%fused_computation.1 | convolution fusion | flops 7552696320 | bytes 20480000 | tf_op jit(solution)/shard_map/dot_general | solution.py:380
  144.0 0.0 copy-start.5
  144.0 58.7 %combine.1 = (bf16[8,40,2560]{2,1,0:T(8,128)(2,1)S(1)}, f32[3,96,1280]{2,1,0:T(8,128)S(1)}) custom-call(bf16[2,2,8,40,2560]{4,3,2,1,0:T(8,128)(2,1)} %bitcast.33, bf16[3,2,96,5120]{3,2,1,0:T(8,128)(2,1)} %bitcast.34), custom_call_target="tpu_custom_call" | custom-call | tf_op jit(solution)/shard_map/combine/pallas_call | solution.py:292
  202.7 0.0 copy-done.5
  202.8 0.5 convolution_convert_fusion.3
  203.3 0.0 copy-start
  203.3 0.0 copy-start.2
  203.4 0.0 copy-start.3
  203.4 0.5 convolution_convert_fusion.4
  203.9 1.2 pad_maximum_fusion
  205.1 0.0 copy-done
  205.1 0.0 copy-done.2
  205.1 0.7 copy-done.3
  205.9 2.8 %divide_subtract_fusion = (f32[3,96,1280]{2,1,0:T(8,128)}, f32[3,96,1280]{2,1,0:T(8,128)}, f32[3,96,1280]{2,1,0:T(8,128)}) fusion(f32[3,96,1280]{2,1,0:T(8,128)S(1)} %copy.13, bf16[3,96,1280]{2,1,0:T(8,128)(2,1)S(1)} %copy-done, f32[3,96,1280]{2,1,0:T(8,128)S(1)} %get-tuple-element.11, f32[3,96,1280]{2,1,0:T(8,128)S(1)} %copy-done.2, ...), kind=kLoop, calls=%fused_computation.17 | loop fusion | flops 5160960 | bytes 11059200 | tf_op jit(solution)/shard_map/sub | solution.py:421
  (5 shorter events, 0.0 us)
Async XLA Ops:
  3.1 4.5 %copy-start.4 = (f32[3,96,10]{1,0,2:T(4,128)S(1)}, f32[3,96,10]{1,0,2:T(4,128)}, u32[]{:S(2)}) copy-start(f32[3,96,10]{1,0,2:T(4,128)} %param.11) | copy-start | bytes 34564
  122.6 2.7 %copy-start.1 = (bf16[3,2,96,5120]{3,2,1,0:T(8,128)(2,1)S(1)}, bf16[3,2,96,5120]{3,2,1,0:T(8,128)(2,1)}, u32[]{:S(2)}) copy-start(bf16[3,2,96,5120]{3,2,1,0:T(8,128)(2,1)} %get-tuple-element.9) | copy-start | bytes 17694724
  125.8 7.9 %slice-start = ((s8[13107200]{0:T(1024)(128)(4,1)}), s8[4194304]{0:T(1024)(128)(4,1)S(1)}, s32[]{:S(2)}) async-start(s8[13107200]{0:T(1024)(128)(4,1)} %bitcast.43), calls=%async_computation | async-start | bytes 8388608
  125.8 7.9 %slice-start.1 = ((s8[13107200]{0:T(1024)(128)(4,1)}), s8[4194304]{0:T(1024)(128)(4,1)S(1)}, s32[]{:S(2)}) async-start(s8[13107200]{0:T(1024)(128)(4,1)} %bitcast.43), calls=%async_computation.1 | async-start | bytes 8388608
  125.8 7.9 %slice-start.2 = ((s8[13107200]{0:T(1024)(128)(4,1)}), s8[4194304]{0:T(1024)(128)(4,1)S(1)}, s32[]{:S(2)}) async-start(s8[13107200]{0:T(1024)(128)(4,1)} %bitcast.43), calls=%async_computation.2 | async-start | bytes 8388608
  125.9 7.9 %slice-start.3 = ((s8[13107200]{0:T(1024)(128)(4,1)}), s8[524288]{0:T(1024)(128)(4,1)S(1)}, s32[]{:S(2)}) async-start(s8[13107200]{0:T(1024)(128)(4,1)} %bitcast.43), calls=%async_computation.3 | async-start | bytes 1048576
  144.0 58.7 %copy-start.5 = (s32[128,1]{0,1:T(1,128)S(1)}, s32[128,1]{0,1:T(1,128)}, u32[]{:S(2)}) copy-start(s32[128,1]{0,1:T(1,128)} %param.9) | copy-start | bytes 1540
  203.3 1.8 copy-start
  203.3 1.8 copy-start.2
  203.4 2.5 %copy-start.3 = (f32[3,96,1280]{2,1,0:T(8,128)S(1)}, f32[3,96,1280]{2,1,0:T(8,128)}, u32[]{:S(2)}) copy-start(f32[3,96,1280]{2,1,0:T(8,128)} %param.13) | copy-start | bytes 4423684

commit v3 on v0

v3 whole, which is shorter than its diff:
```python
import jax
import jax.numpy as jnp
from jax import lax
from jax.experimental import pallas as pl
from jax.experimental.pallas import tpu as pltpu
from jax.sharding import PartitionSpec as P

MESH = pl.DeviceIdType.MESH
QB = 128
NZ, NX, NY = 8, 4, 4
CAP = 20
MAIN, REST = 16, 4
PARTS = 4
ROWS = 4 * CAP
ORDER = (0, 1, 7, 2, 6, 3, 5, 4)
HBM = pl.BlockSpec(memory_space=pltpu.HBM)
VMEM = pl.BlockSpec(memory_space=pltpu.VMEM)

BETA_ONE = 0.9
BETA_TWO = 0.999
LEARNING_RATE = 0.01
ADAM_EPS = 1e-08
STEP_COUNT = 10

f32, bf16 = jnp.float32, jnp.bfloat16


def place():
    dev = lax.axis_index("dev")
    return lax.axis_index("group"), dev // 8, (dev // 2) % 4, dev % 2


def device(y, z, x, c):
    return (y, (z * NX + x) * 2 + c)


def along_z(k):
    y, z, x, c = place()
    return device(y, (z + k) % NZ, x, c)


def along_y(k):
    y, z, x, c = place()
    return device((y + k) % NY, z, x, c)


def token_pair():
    y, z, x, c = place()
    return device(y, z, x + 1 - 2 * (x % 2), c)


def weight_pair():
    y, z, x, c = place()
    return device(y, z, 3 - x, c)


def other_core():
    y, z, x, c = place()
    return device(y, z, x, 1 - c)


def greet(peers):
    barrier = pltpu.get_barrier_semaphore()
    for peer in peers:
        pl.semaphore_signal(barrier, inc=1, device_id=peer, device_id_type=MESH)
    pl.semaphore_wait(barrier, len(peers))


def remote(src, dst, send, recv, peer):
    copy = pltpu.make_async_remote_copy(src, dst, send, recv, device_id=peer, device_id_type=MESH)
    copy.start()
    return copy


def quarter_rows(part, rows_first):
    shape = (4 * MAIN, MAIN) if rows_first else (MAIN, 4 * MAIN)
    row = lax.broadcasted_iota(jnp.int32, shape, 0 if rows_first else 1)
    slot = lax.broadcasted_iota(jnp.int32, shape, 1 if rows_first else 0)
    source, inner = slot // REST, slot % REST
    return jnp.where(row == source * MAIN + part * REST + inner, 1.0, 0.0).astype(bf16)


def expert_kernel(
    slabs, owned, returned, gradient,
    inbound, weights, pre, signals, terms, rest, grads, crossed, paired,
    from_x, block, from_y, from_y_block, part, given,
    z_send, z_recv, x_send, x_recv, c_send, c_recv, w_send, w_recv,
    e_send, e_recv, p_send, p_recv, r_send, r_recv,
    g_send, g_recv, y_send, y_recv, b_send, b_recv, t_send, t_recv, local,
):
    y = lax.axis_index("group")
    stored, width = owned.shape[1:]
    features = weights.shape[3]
    units = 2 * stored
    half = stored // 2
    low, high = pl.ds(0, half), pl.ds(half, half)

    def columns(k):
        return pl.ds(pl.multiple_of((y + k) % NY * width, width), width)

    mine = columns(0)

    def source_rows(number):
        return pl.ds(number * MAIN, MAIN)

    greet(
        [along_z(k) for k in range(1, NZ)]
        + [along_y(k) for k in range(1, NY)]
        + [token_pair(), weight_pair(), other_core()]
    )

    keep_rows = pltpu.make_async_copy(
        slabs.at[0], inbound.at[:, 0, source_rows(0)], local.at[0]
    )
    keep_rows.start()
    to_z = [None]
    def launch(at):
        k = ORDER[at]
        to_z.append(
            remote(
                slabs.at[k],
                inbound.at[:, at, source_rows(0)],
                z_send.at[at],
                z_recv.at[at],
                along_z(k),
            )
        )
    for at in range(1, 5):
        launch(at)
    to_partner = remote(owned, weights.at[:, 1, :, mine], w_send.at[0], w_recv.at[0], weight_pair())
    keep_weights = pltpu.make_async_copy(owned, weights.at[:, 0, :, mine], local.at[1])
    keep_weights.start()
    to_y = [
        remote(owned, weights.at[:, 0, :, mine], w_send.at[k], w_recv.at[k], along_y(k))
        for k in range(1, NY)
    ]
    to_x, to_c = [], []

    def spread(at):
        own = inbound.at[:, at, source_rows(0)]
        to_x.append(
            remote(
                own,
                inbound.at[:, at, source_rows(1)],
                x_send.at[at],
                x_recv.at[at],
                token_pair(),
            )
        )
        to_c.append(
            [
                remote(
                    own,
                    inbound.at[:, at, source_rows(2)],
                    c_send.at[0, at],
                    c_recv.at[0, at],
                    other_core(),
                )
            ]
        )

    def cross(at):
        to_x[at].wait_recv()
        to_c[at].append(
            remote(
                inbound.at[:, at, source_rows(1)],
                inbound.at[:, at, source_rows(3)],
                c_send.at[1, at],
                c_recv.at[1, at],
                other_core(),
            )
        )

    def arrive(at):
        to_z[at].wait_recv()
        spread(at)

    def weights_on():
        to_partner.wait_recv()
        for k in range(1, NY):
            to_y.append(
                remote(
                    weights.at[:, 1, :, mine],
                    weights.at[:, 1, :, mine],
                    w_send.at[NY - 1 + k],
                    w_recv.at[NY - 1 + k],
                    along_y(k),
                )
            )

    def work(first, count):
        for at in range(first, first + count):
            for copy in to_c[at]:
                copy.wait_recv()
        rows = count * ROWS
        stretch = pl.ds(first * ROWS, rows)
        pre[:, :rows] = jnp.zeros((3, rows, units), f32)

        def project(number, carry):
            cut = pl.ds(pl.multiple_of(number * width, width), width)
            pick = quarter_rows(number, False)
            for at in range(first, first + count):
                for t in range(2):
                    inbound[t, at, 4 * MAIN :, cut] = jnp.dot(
                        pick, inbound[t, at, : 4 * MAIN, features:], preferred_element_type=f32
                    ).astype(bf16)
            for m in range(3):
                pre[m, :rows] += lax.dot_general(
                    inbound[m // 2, first : first + count, :, cut].reshape(rows, width),
                    weights[m, :, :, cut].reshape(units, width),
                    (((1,), (1,)), ((), ())),
                    preferred_element_type=f32,
                )
            return carry

        lax.fori_loop(0, PARTS, project, 0)
        gate, up, hidden_cot = pre[0, :rows], pre[1, :rows], pre[2, :rows]
        sig = jax.nn.sigmoid(gate)
        activated = gate * sig
        signals[2, stretch] = (activated * up).astype(bf16)
        signals[0, stretch] = (hidden_cot * up * sig * (1.0 + gate * (1.0 - sig))).astype(bf16)
        signals[1, stretch] = (hidden_cot * activated).astype(bf16)
        rest[...] = jnp.zeros(rest.shape, f32)

        def give_back(number, carry):
            cut = pl.ds(pl.multiple_of(number * width, width), width)
            place_rows = quarter_rows(number, True)
            term = (
                jnp.dot(
                    signals[0, stretch],
                    weights[0, :, :, cut].reshape(units, width),
                    preferred_element_type=f32,
                )
                + jnp.dot(
                    signals[1, stretch],
                    weights[1, :, :, cut].reshape(units, width),
                    preferred_element_type=f32,
                )
            ).astype(bf16)
            for i in range(count):
                one = term[i * ROWS : (i + 1) * ROWS]
                terms[first + i, :, :, cut] = one[: 4 * MAIN].reshape(4, MAIN, width)
                rest[i] += jnp.dot(place_rows, one[4 * MAIN :], preferred_element_type=f32)
            return carry

        lax.fori_loop(0, PARTS, give_back, 0)
        for i in range(count):
            terms[first + i, :, :, features:] = rest[i].astype(bf16).reshape(4, MAIN, width)
        for at in range(first, first + count):
            to_e[at] = remote(
                terms.at[at, pl.ds(2, 2)], crossed.at[at], e_send.at[at], e_recv.at[at], other_core()
            )

    to_e, to_p, to_r = {}, {}, {}

    def fold(at):
        to_e[at].wait_recv()
        for col in (1, 0):
            terms[at, col] = (terms[at, col].astype(f32) + crossed[at, col].astype(f32)).astype(bf16)
            if col:
                to_p[at] = remote(
                    terms.at[at, 1], paired.at[at], p_send.at[at], p_recv.at[at], token_pair()
                )

    def back(at):
        to_p[at].wait_recv()
        terms[at, 0] = (terms[at, 0].astype(f32) + paired[at].astype(f32)).astype(bf16)
        k = ORDER[at]
        if k:
            to_r[at] = remote(
                terms.at[at, 0], returned.at[k], r_send.at[at], r_recv.at[at], along_z(NZ - k)
            )

    to_g, to_s, to_b, to_t = [], [], [], []

    def differentiate(m):
        def columns_of(number, carry):
            cut = pl.ds(pl.multiple_of(number * (width // 2), width // 2), width // 2)
            grads[m, :, :, cut] = (
                lax.dot_general(
                    signals[m],
                    inbound[m // 2, :, :, cut].reshape(NZ * ROWS, width // 2),
                    (((0,), (0,)), ((), ())),
                    preferred_element_type=f32,
                )
                .astype(bf16)
                .reshape(2, stored, width // 2)
            )
            return carry

        lax.fori_loop(0, 2 * PARTS, columns_of, 0)
        to_g.append(
            remote(grads.at[m, 1, high], from_x.at[m], g_send.at[m], g_recv.at[m], weight_pair())
        )
        for k in range(1, NY):
            to_s.append(
                remote(
                    grads.at[m, :, low, columns(k)],
                    from_y.at[k - 1, m],
                    y_send.at[m, k],
                    y_recv.at[m, k],
                    along_y(k),
                )
            )

    def through(m):
        to_g[m].wait_recv()
        block[m] = (grads[m, 0, high].astype(f32) + from_x[m].astype(f32)).astype(bf16)
        for k in range(1, NY):
            to_b.append(
                remote(
                    block.at[m, :, columns(k)],
                    from_y_block.at[k - 1, m],
                    b_send.at[m, k],
                    b_recv.at[m, k],
                    along_y(k),
                )
            )

    def gather(m):
        for copy in to_s[m * (NY - 1) : (m + 1) * (NY - 1)]:
            copy.wait_recv()
        for b in (1, 0):
            total = grads[m, b, low, mine].astype(f32)
            for k in range(NY - 1):
                total = total + from_y[k, m, b].astype(f32)
            if b:
                part[m] = total.astype(bf16)
                to_t.append(
                    remote(part.at[m], given.at[m], t_send.at[m], t_recv.at[m], weight_pair())
                )
            else:
                gradient[m, low] = total

    def finish(m):
        for copy in to_b[m * (NY - 1) : (m + 1) * (NY - 1)]:
            copy.wait_recv()
        total = block[m, :, mine].astype(f32)
        for k in range(NY - 1):
            total = total + from_y_block[k, m].astype(f32)
        gradient[m, high] = total
        to_t[m].wait_recv()
        gradient[m, low] = gradient[m, low] + given[m].astype(f32)

    keep_rows.wait()
    spread(0)
    weights_on()
    for at in range(1, 6):
        arrive(at)
        if at + 4 < NZ:
            launch(at + 4)
        cross(at - 1)
    keep_weights.wait()
    for copy in to_y:
        copy.wait_recv()
    arrive(6)
    cross(5)
    work(0, 5)
    arrive(7)
    cross(6)
    work(5, 2)
    cross(7)
    work(7, 1)
    FAR = (7, 6, 5, 4, 3, 2, 1, 0)
    for at in FAR:
        fold(at)
    for m in range(3):
        differentiate(m)
    back(FAR[0])
    back(FAR[1])
    through(0)
    back(FAR[2])
    gather(0)
    back(FAR[3])
    through(1)
    back(FAR[4])
    gather(1)
    back(FAR[5])
    back(FAR[6])
    through(2)
    back(FAR[7])
    keep = pltpu.make_async_copy(terms.at[0, 0], returned.at[0], local.at[0])
    keep.start()
    gather(2)
    for m in range(3):
        finish(m)
    keep.wait()
    for at in range(NZ):
        to_e[at].wait_send()
        to_p[at].wait_send()
        to_x[at].wait_send()
        for copy in to_c[at]:
            copy.wait_send()
        if at:
            to_z[at].wait_send()
            to_r[at].wait()
    to_partner.wait_send()
    for copy in to_y + to_g + to_s + to_b + to_t:
        copy.wait_send()


def expert_step(slabs, owned):
    _, _, _, long = slabs.shape
    _, stored, width = owned.shape
    features = NY * width
    units, half = 2 * stored, stored // 2
    dma = pltpu.SemaphoreType.DMA
    return pl.pallas_call(
        expert_kernel,
        out_shape=(
            jax.ShapeDtypeStruct((NZ, MAIN, long), bf16),
            jax.ShapeDtypeStruct((3, stored, width), f32),
        ),
        in_specs=[HBM, HBM],
        out_specs=(HBM, VMEM),
        scratch_shapes=[
            pltpu.VMEM((2, NZ, ROWS, long), bf16),
            pltpu.VMEM((3, 2, stored, features), bf16),
            pltpu.VMEM((3, 5 * ROWS, units), f32),
            pltpu.VMEM((3, NZ * ROWS, units), bf16),
            pltpu.VMEM((NZ, 4, MAIN, long), bf16),
            pltpu.VMEM((5, 4 * MAIN, width), f32),
            pltpu.VMEM((3, 2, stored, features), bf16),
            pltpu.VMEM((NZ, 2, MAIN, long), bf16),
            pltpu.VMEM((NZ, MAIN, long), bf16),
            pltpu.VMEM((3, half, features), bf16),
            pltpu.VMEM((3, half, features), bf16),
            pltpu.VMEM((NY - 1, 3, 2, half, width), bf16),
            pltpu.VMEM((NY - 1, 3, half, width), bf16),
            pltpu.VMEM((3, half, width), bf16),
            pltpu.VMEM((3, half, width), bf16),
        ]
        + [dma((NZ,))] * 4
        + [dma((2, NZ))] * 2
        + [dma((2 * NY - 1,))] * 2
        + [dma((NZ,))] * 6
        + [dma((3,))] * 2
        + [dma((3, NY))] * 4
        + [dma((3,))] * 2
        + [dma((2,))],
        compiler_params=pltpu.CompilerParams(
            collective_id=0, has_side_effects=True, vmem_limit_bytes=60 << 20
        ),
        cost_estimate=pl.CostEstimate(flops=10 * 10**9, bytes_accessed=10**8, transcendentals=0),
        name="expert_step",
    )(slabs, owned)


def shards(tokens, cotangent, routes, codes, scales, first_moment, second_moment):
    row_count, features = tokens.shape
    stored, width = codes.shape[1:]
    _, z, _, _ = place()
    owned_full = codes.astype(f32) * jnp.repeat(scales, QB, axis=2)
    owned = owned_full.astype(bf16)

    route_ids = routes[:, 0]
    matches = route_ids[:, None] == jnp.arange(NZ, dtype=jnp.int32)[None, :]
    counted = matches.astype(jnp.int32)
    earlier = jnp.cumsum(counted, axis=0) - counted
    position = jnp.sum(jnp.where(matches, earlier, 0), axis=1)
    ahead = (route_ids - z + NZ) % NZ
    main_slot = jnp.where(position < MAIN, ahead * MAIN + position, -1)

    def rest_slot(part):
        return jnp.where(position < MAIN, -1, ahead * MAIN + part * REST + position - MAIN)

    slots = jnp.arange(NZ * MAIN, dtype=jnp.int32)

    def pack(values):
        main = jnp.dot(
            (slots[:, None] == main_slot[None, :]).astype(bf16), values, preferred_element_type=f32
        )
        chosen = jnp.concatenate(
            [slots[:, None] == rest_slot(part)[None, :] for part in range(PARTS)], axis=1
        ).astype(bf16)
        quarters = jnp.concatenate(
            [values[:, part * width : (part + 1) * width] for part in range(PARTS)], axis=0
        )
        rest = jnp.dot(chosen, quarters, preferred_element_type=f32)
        packed = jnp.concatenate([main.astype(bf16), rest.astype(bf16)], axis=1)
        return packed.reshape(NZ, MAIN, features + width)

    slabs = jnp.stack([pack(tokens), pack(cotangent)], axis=1)
    returned, gradient = expert_step(slabs, owned)
    flat = returned.reshape(NZ * MAIN, features + width)
    grad_tokens = jnp.concatenate(
        [
            jnp.dot(
                jnp.concatenate(
                    [
                        main_slot[:, None] == slots[None, :],
                        rest_slot(part)[:, None] == slots[None, :],
                    ],
                    axis=1,
                ).astype(bf16),
                jnp.concatenate(
                    [flat[:, part * width : (part + 1) * width], flat[:, features:]], axis=0
                ),
                preferred_element_type=f32,
            ).astype(bf16)
            for part in range(PARTS)
        ],
        axis=1,
    )
    new_first = BETA_ONE * first_moment + (1.0 - BETA_ONE) * gradient
    new_second = BETA_TWO * second_moment + (1.0 - BETA_TWO) * gradient * gradient
    first_fix = 1.0 - BETA_ONE**STEP_COUNT
    second_fix = 1.0 - BETA_TWO**STEP_COUNT
    new_weights = owned_full - LEARNING_RATE * (new_first / first_fix) / (
        jnp.sqrt(new_second / second_fix) + ADAM_EPS
    )
    return (grad_tokens, new_weights, new_first, new_second)


def solution(mesh):
    stored = P(None, "dev", "group")
    spread = P(("group", "dev"), None)
    return jax.shard_map(
        shards,
        mesh=mesh,
        in_specs=(spread, spread, spread, stored, stored, stored, stored),
        out_specs=(spread, stored, stored, stored),
        check_vma=False,
    )
```

time: 824 us -> 189 us (0.23)
  waiting for transfers between devices: 645 us -> 0 us
  Pallas kernels: 0 us -> 167 us
  local copies, waits for them, and re-layouts: 58.8 us -> 5.39 us
  matrix products: 39.3 us -> 2.69 us
  starting transfers between devices: 34.8 us -> 0 us
  other arithmetic: 28.2 us -> 13.4 us
  between operations: 14.3 us -> 0.86 us
    all_to_all x3 -> x0, waiting for transfers between devices: 565 us -> none  [the longest x1 227 us: shards(): lax.all_to_all(replicate(send_rows), 'dev', split_axis=0, concat_axis=0,...]
    pallas_call x0 -> x1, Pallas kernels: none -> 167 us  [expert_step(): pl.pallas_call(expert_kernel, out_shape=(jax.ShapeDtypeStruct((NZ, MAIN,...]
    all_gather x1 -> x0, waiting for transfers between devices: 41.7 us -> none  [shards(): gathered = lax.all_gather(owned, 'group', axis=2, tiled=True)]
    all_to_all x3 -> x0, local copies, waits for them, and re-layouts: 38.5 us -> none  [the longest x1 12.9 us: shards(): lax.all_to_all(replicate(send_cot), 'dev', split_axis=0, concat_axis=0, t...]
    dot_general x10 -> x8, matrix products: 39.3 us -> 2.69 us  [the longest x4 1.02 us: shards(): jnp.dot(jnp.concatenate([main_slot[:, None] == slots[None, :], rest_slot(...]
    all_to_all x3 -> x0, starting transfers between devices: 33.3 us -> none  [the longest x1 13.2 us: shards(): lax.all_to_all(replicate(send_rows), 'dev', split_axis=0, concat_axis=0,...]
    reduce_scatter x1 -> x0, waiting for transfers between devices: 31.2 us -> none  [shards(): lax.psum_scatter(jnp.stack([gate_grad, upward_grad, down_grad]).astype(jn...]
    broadcast_in_dim x5 -> x1, local copies, waits for them, and re-layouts: 15.6 us -> 0.13 us  [shards(): owned_full = codes.astype(f32) * jnp.repeat(scales, QB, axis=2)]
  transfers between devices with their start and end apart: 7 -> 0, of which waited for: 7 -> 0; matrix products, arithmetic and copies ran while one was open for 5% -> 0% of each run, Pallas kernels for 0% -> 0%
where the time goes in v3:
time: 189 us
  Pallas kernels  167 us (88%)
  other arithmetic  13.4 us (7%)
  local copies, waits for them, and re-layouts  5.39 us (3%)
  matrix products  2.69 us (1%)
    pallas_call x1, Pallas kernels, expert_step(): pl.pallas_call(expert_kernel, out_shape=(jax.ShapeDtypeStruct((NZ, MAIN,...  167 us
    sub x1, other arithmetic, shards(): owned_full - LEARNING_RATE * (new_first / first_fix) / (jnp.sqrt(new_seco...  5.09 us

profile of v3, /device:TPU:1, one launch (start us, length us, event | category | flops | bytes accessed | tf_op | source)
XLA Modules:
  0.0 189.1 jit_solution(13130374318691301519)
XLA Ops:
  0.6 0.7 fusion.24
  1.4 0.2 reduce_window_sum.11
  1.6 0.8 select_reduce_fusion
  2.4 0.7 broadcast_select_fusion
  3.1 1.4 fusion.54
  4.5 0.0 copy-start
  4.5 0.3 convolution_convert_fusion.7
  4.9 1.0 copy-done
  5.8 0.5 convolution_convert_fusion.1
  6.3 0.0 copy-start.1
  6.3 0.1 pad_maximum_fusion.1
  6.5 1.2 copy-done.1
  7.6 0.1 fusion.55
  7.7 0.3 convolution_convert_fusion.6
  8.1 0.5 convolution_convert_fusion
  8.6 0.1 pad_maximum_fusion.2
  8.7 0.0 copy-start.4
  8.7 2.0 %pad_maximum_fusion.slabs = bf16[8,2,16,6400]{3,2,1,0:T(8,128)(2,1)} fusion(bf16[8,1,16,6400]{3,2,1,0:T(8,128)(2,1)S(1)} %bitcast.59, bf16[8,1,16,6400]{3,2,1,0:T(8,128)(2,1)S(1)} %bitcast.58), kind=kLoop, calls=%fused_computation.2 | loop fusion | flops 1638400 | bytes 6553600 | tf_op jit(solution)/shard_map/stack | solution.py:483
  10.7 0.0 copy-done.4
  10.7 0.1 broadcast_in_dim.28
  10.8 1.0 copy.13
  11.8 2.1 %fusion.15.owned = bf16[3,96,1280]{2,1,0:T(8,128)(2,1)} fusion(f32[3,96,1280]{2,1,0:T(8,128)S(1)} %copy.13, bf16[3,96,1280]{2,1,0:T(8,128)(2,1)} %param.10), kind=kLoop, calls=%fused_computation.31 | loop fusion | flops 1105920 | bytes 2949120 | tf_op jit(solution)/shard_map/convert_element_type | solution.py:454
  14.0 0.0 copy-start.2
  14.0 166.8 %expert_step.1 = (bf16[8,16,6400]{2,1,0:T(8,128)(2,1)}, f32[3,96,1280]{2,1,0:T(8,128)}) custom-call(bf16[8,2,16,6400]{3,2,1,0:T(8,128)(2,1)} %pad_maximum_fusion.slabs, bf16[3,96,1280]{2,1,0:T(8,128)(2,1)} %fusion.15.owned), custom_call_target="tpu_custom_call" | custom-call | flops 10000000000 | bytes 100000000 | tf_op jit(solution)/shard_map/expert_step/pallas_call | solution.py:408
  180.8 0.0 copy-done.2
  180.8 0.0 copy-start.3
  180.8 5.1 %divide_subtract_fusion = (f32[3,96,1280]{2,1,0:T(8,128)}, f32[3,96,1280]{2,1,0:T(8,128)}, f32[3,96,1280]{2,1,0:T(8,128)}) fusion(f32[3,96,1280]{2,1,0:T(8,128)S(1)} %copy.13, bf16[3,96,1280]{2,1,0:T(8,128)(2,1)S(1)} %copy-done.2, f32[3,96,1280]{2,1,0:T(8,128)} %get-tuple-element.7, f32[3,96,1280]{2,1,0:T(8,128)} %param.12, f32[3,96,1280]{2,1,0:T(8,128)} %param.13), kind=kLoop, calls=%fused_computation.13 | loop fusion | flops 5160960 | bytes 11059200 | tf_op jit(solution)/shard_map/sub | solution.py:509
  185.9 0.0 copy-done.3
  185.9 0.0 copy-start.5
  185.9 0.1 fusion.53
  186.0 0.5 copy-done.5
  186.6 0.1 iota_compare_fusion.2
  186.7 0.1 iota_compare_fusion.10
  186.8 0.3 convolution_convert_fusion.5
  187.0 0.3 convolution_convert_fusion.4
  187.3 0.1 iota_compare_fusion
  187.4 0.3 convolution_convert_fusion.3
  187.7 0.3 convolution_convert_fusion.2
  187.9 1.2 pad_maximum_fusion.3
  (6 shorter events, 0.1 us)
Async XLA Ops:
  4.5 1.3 copy-start
  6.3 1.3 copy-start.1
  8.7 2.0 %copy-start.4 = (f32[3,96,10]{1,0,2:T(4,128)S(1)}, f32[3,96,10]{1,0,2:T(4,128)}, u32[]{:S(2)}) copy-start(f32[3,96,10]{1,0,2:T(4,128)} %param.11) | copy-start | bytes 34564
  14.0 166.8 %copy-start.2 = (bf16[3,96,1280]{2,1,0:T(8,128)(2,1)S(1)}, bf16[3,96,1280]{2,1,0:T(8,128)(2,1)}, u32[]{:S(2)}) copy-start(bf16[3,96,1280]{2,1,0:T(8,128)(2,1)} %param.10) | copy-start | bytes 2211844
  180.8 5.1 %copy-start.3 = (bf16[8,16,6400]{2,1,0:T(8,128)(2,1)S(1)}, bf16[8,16,6400]{2,1,0:T(8,128)(2,1)}, u32[]{:S(2)}) copy-start(bf16[8,16,6400]{2,1,0:T(8,128)(2,1)} %get-tuple-element.6) | copy-start | bytes 4915204
  185.9 0.7 copy-start.5

commit v4 on v3

--- a/solution.py
+++ b/solution.py
@@ -59,13 +59,6 @@
     return device(y, z, x, 1 - c)
 
 
-def greet(peers):
-    barrier = pltpu.get_barrier_semaphore()
-    for peer in peers:
-        pl.semaphore_signal(barrier, inc=1, device_id=peer, device_id_type=MESH)
-    pl.semaphore_wait(barrier, len(peers))
-
-
 def remote(src, dst, send, recv, peer):
     copy = pltpu.make_async_remote_copy(src, dst, send, recv, device_id=peer, device_id_type=MESH)
     copy.start()
@@ -81,16 +74,17 @@
 
 
 def expert_kernel(
-    slabs, owned, returned, gradient,
-    inbound, weights, pre, signals, terms, rest, grads, crossed, paired,
+    tokens, cotangent, routes, codes, scales, token_grads, gradient,
+    slabs, owned, returned, picks, unpicks, inbound, weights, pre, signals, terms, rest, grads, crossed, paired,
     from_x, block, from_y, from_y_block, part, given,
     z_send, z_recv, x_send, x_recv, c_send, c_recv, w_send, w_recv,
     e_send, e_recv, p_send, p_recv, r_send, r_recv,
-    g_send, g_recv, y_send, y_recv, b_send, b_recv, t_send, t_recv, local,
+    g_send, g_recv, y_send, y_recv, b_send, b_recv, t_send, t_recv, local, load,
 ):
     y = lax.axis_index("group")
     stored, width = owned.shape[1:]
     features = weights.shape[3]
+    tail = pl.ds(features, width)
     units = 2 * stored
     half = stored // 2
     low, high = pl.ds(0, half), pl.ds(half, half)
@@ -103,12 +97,74 @@
     def source_rows(number):
         return pl.ds(number * MAIN, MAIN)
 
-    greet(
+    peers = (
         [along_z(k) for k in range(1, NZ)]
         + [along_y(k) for k in range(1, NY)]
         + [token_pair(), weight_pair(), other_core()]
     )
-
+    barrier = pltpu.get_barrier_semaphore()
+    for peer in peers:
+        pl.semaphore_signal(barrier, inc=1, device_id=peer, device_id_type=MESH)
+
+    loads = []
+    for t, source in enumerate((tokens, cotangent)):
+        loads.append(
+            pltpu.make_async_copy(
+                source, terms.at[pl.ds(2 * t, 2), :, :, pl.ds(0, features)], load.at[t]
+            )
+        )
+        loads[t].start()
+    for b in range(scales.shape[2]):
+        cut = pl.ds(b * QB, QB)
+        owned[:, :, cut] = (codes[:, :, cut].astype(f32) * scales[:, :, b : b + 1]).astype(bf16)
+
+    count = routes.shape[1]
+    _, z, _, _ = place()
+    row_range = lax.broadcasted_iota(jnp.int32, (count, count), 0)
+    column_range = lax.broadcasted_iota(jnp.int32, (count, count), 1)
+    before = jnp.where(row_range < column_range, 1.0, 0.0).astype(bf16)
+    matches = lax.broadcasted_iota(jnp.int32, (MAIN, count), 0) == routes[...]
+    earlier = jnp.dot(
+        jnp.where(matches, 1.0, 0.0).astype(bf16), before, preferred_element_type=f32
+    )
+    position = jnp.sum(jnp.where(matches, earlier, 0.0), axis=0, keepdims=True).astype(jnp.int32)
+    first_slot = (routes[...] - z + NZ) % NZ * MAIN
+    in_main = position < MAIN
+    for number in range(PARTS + 1):
+        if number < PARTS:
+            slot = jnp.where(in_main, -1, first_slot + number * REST + position - MAIN)
+        else:
+            slot = jnp.where(in_main, first_slot + position, -1)
+        pick = jnp.where(row_range == slot, 1.0, 0.0)
+        picks[number] = pick.astype(bf16)
+        unpicks[number] = pick.T.astype(bf16)
+
+    pl.semaphore_wait(barrier, len(peers))
+
+    to_partner = remote(owned, weights.at[:, 1, :, mine], w_send.at[0], w_recv.at[0], weight_pair())
+    keep_weights = pltpu.make_async_copy(owned, weights.at[:, 0, :, mine], local.at[1])
+    keep_weights.start()
+    to_y = [
+        remote(owned, weights.at[:, 0, :, mine], w_send.at[k], w_recv.at[k], along_y(k))
+        for k in range(1, NY)
+    ]
+    for t in range(2):
+        loads[t].wait()
+
+        def pack(number, carry):
+            cut = pl.ds(pl.multiple_of(number * width, width), width)
+            values = terms[2 * t : 2 * t + 2, :, :, cut].reshape(count, width)
+            slabs[:, t, :, cut] = (
+                jnp.dot(picks[PARTS], values, preferred_element_type=f32)
+                .astype(bf16)
+                .reshape(NZ, MAIN, width)
+            )
+            left = jnp.dot(picks[number], values, preferred_element_type=f32)
+            slabs[:, t, :, tail] = slabs[:, t, :, tail] + left.astype(bf16).reshape(NZ, MAIN, width)
+            return carry
+
+        slabs[:, t, :, tail] = jnp.zeros((NZ, MAIN, width), bf16)
+        lax.fori_loop(0, PARTS, pack, 0)
     keep_rows = pltpu.make_async_copy(
         slabs.at[0], inbound.at[:, 0, source_rows(0)], local.at[0]
     )
@@ -127,13 +183,6 @@
         )
     for at in range(1, 5):
         launch(at)
-    to_partner = remote(owned, weights.at[:, 1, :, mine], w_send.at[0], w_recv.at[0], weight_pair())
-    keep_weights = pltpu.make_async_copy(owned, weights.at[:, 0, :, mine], local.at[1])
-    keep_weights.start()
-    to_y = [
-        remote(owned, weights.at[:, 0, :, mine], w_send.at[k], w_recv.at[k], along_y(k))
-        for k in range(1, NY)
-    ]
     to_x, to_c = [], []
 
     def spread(at):
@@ -188,15 +237,12 @@
                 )
             )
 
-    def work(first, count):
+    def unpack_rest(first, count):
         for at in range(first, first + count):
             for copy in to_c[at]:
                 copy.wait_recv()
-        rows = count * ROWS
-        stretch = pl.ds(first * ROWS, rows)
-        pre[:, :rows] = jnp.zeros((3, rows, units), f32)
-
-        def project(number, carry):
+
+        def unpack(number, carry):
             cut = pl.ds(pl.multiple_of(number * width, width), width)
             pick = quarter_rows(number, False)
             for at in range(first, first + count):
@@ -204,25 +250,40 @@
                     inbound[t, at, 4 * MAIN :, cut] = jnp.dot(
                         pick, inbound[t, at, : 4 * MAIN, features:], preferred_element_type=f32
                     ).astype(bf16)
+            return carry
+
+        lax.fori_loop(0, PARTS, unpack, 0)
+
+    def project(first, count, turns):
+        rows = count * ROWS
+        stretch = pl.ds(first * ROWS, rows)
+        for k in turns:
+            cut = columns(NY - k)
             for m in range(3):
-                pre[m, :rows] += lax.dot_general(
+                term = lax.dot_general(
                     inbound[m // 2, first : first + count, :, cut].reshape(rows, width),
                     weights[m, :, :, cut].reshape(units, width),
                     (((1,), (1,)), ((), ())),
                     preferred_element_type=f32,
                 )
-            return carry
-
-        lax.fori_loop(0, PARTS, project, 0)
-        gate, up, hidden_cot = pre[0, :rows], pre[1, :rows], pre[2, :rows]
+                if k == 0:
+                    pre[m, stretch] = term
+                else:
+                    pre[m, stretch] += term
+
+    def activate(first, count):
+        stretch = pl.ds(first * ROWS, count * ROWS)
+        gate, up, hidden_cot = pre[0, stretch], pre[1, stretch], pre[2, stretch]
         sig = jax.nn.sigmoid(gate)
         activated = gate * sig
         signals[2, stretch] = (activated * up).astype(bf16)
         signals[0, stretch] = (hidden_cot * up * sig * (1.0 + gate * (1.0 - sig))).astype(bf16)
         signals[1, stretch] = (hidden_cot * activated).astype(bf16)
-        rest[...] = jnp.zeros(rest.shape, f32)
-
-        def give_back(number, carry):
+
+    def give_back(first, count, low_part, high_part):
+        stretch = pl.ds(first * ROWS, count * ROWS)
+
+        def one_part(number, carry):
             cut = pl.ds(pl.multiple_of(number * width, width), width)
             place_rows = quarter_rows(number, True)
             term = (
@@ -243,13 +304,27 @@
                 rest[i] += jnp.dot(place_rows, one[4 * MAIN :], preferred_element_type=f32)
             return carry
 
-        lax.fori_loop(0, PARTS, give_back, 0)
-        for i in range(count):
-            terms[first + i, :, :, features:] = rest[i].astype(bf16).reshape(4, MAIN, width)
-        for at in range(first, first + count):
-            to_e[at] = remote(
-                terms.at[at, pl.ds(2, 2)], crossed.at[at], e_send.at[at], e_recv.at[at], other_core()
-            )
+        if low_part == 0:
+            rest[:count] = jnp.zeros((count,) + rest.shape[1:], f32)
+        lax.fori_loop(low_part, high_part, one_part, 0)
+        if high_part == PARTS:
+            for i in range(count):
+                terms[first + i, :, :, features:] = rest[i].astype(bf16).reshape(4, MAIN, width)
+            for at in range(first, first + count):
+                to_e[at] = remote(
+                    terms.at[at, pl.ds(2, 2)],
+                    crossed.at[at],
+                    e_send.at[at],
+                    e_recv.at[at],
+                    other_core(),
+                )
+
+    def weights_of(k):
+        if k:
+            to_y[k - 1].wait_recv()
+            to_y[NY - 2 + k].wait_recv()
+        else:
+            keep_weights.wait()
 
     to_e, to_p, to_r = {}, {}, {}
 
@@ -264,9 +339,12 @@
 
     def back(at):
         to_p[at].wait_recv()
-        terms[at, 0] = (terms[at, 0].astype(f32) + paired[at].astype(f32)).astype(bf16)
+        total = (terms[at, 0].astype(f32) + paired[at].astype(f32)).astype(bf16)
         k = ORDER[at]
-        if k:
+        if k == 0:
+            returned[0] = total
+        else:
+            terms[at, 0] = total
             to_r[at] = remote(
                 terms.at[at, 0], returned.at[k], r_send.at[at], r_recv.at[at], along_z(NZ - k)
             )
@@ -344,28 +422,52 @@
 
     keep_rows.wait()
     spread(0)
+    arrive(1)
+    launch(5)
+    cross(0)
+    arrive(2)
+    launch(6)
     weights_on()
-    for at in range(1, 6):
-        arrive(at)
-        if at + 4 < NZ:
-            launch(at + 4)
-        cross(at - 1)
-    keep_weights.wait()
-    for copy in to_y:
-        copy.wait_recv()
+    cross(1)
+    cross(2)
+    arrive(3)
+    launch(7)
+    arrive(4)
+    cross(3)
+    cross(4)
+    unpack_rest(0, 5)
+    weights_of(0)
+    project(0, 5, (0,))
+    weights_of(1)
+    project(0, 5, (1,))
+    arrive(5)
+    weights_of(3)
+    project(0, 5, (3,))
     arrive(6)
     cross(5)
-    work(0, 5)
+    weights_of(2)
+    project(0, 5, (2,))
+    activate(0, 5)
+    cross(6)
+    give_back(0, 5, 0, 2)
     arrive(7)
-    cross(6)
-    work(5, 2)
+    give_back(0, 5, 2, 4)
+    unpack_rest(5, 2)
+    project(5, 2, (0, 1, 3, 2))
+    activate(5, 2)
+    give_back(5, 2, 0, 4)
     cross(7)
-    work(7, 1)
-    FAR = (7, 6, 5, 4, 3, 2, 1, 0)
-    for at in FAR:
+    unpack_rest(7, 1)
+    project(7, 1, (0, 1, 3, 2))
+    activate(7, 1)
+    FAR = (6, 5, 7, 4, 3, 2, 1, 0)
+    for at in (6, 5):
         fold(at)
     for m in range(3):
         differentiate(m)
+    give_back(7, 1, 0, 4)
+    for at in FAR[2:]:
+        fold(at)
     back(FAR[0])
     back(FAR[1])
     through(0)
@@ -379,12 +481,29 @@
     back(FAR[6])
     through(2)
     back(FAR[7])
-    keep = pltpu.make_async_copy(terms.at[0, 0], returned.at[0], local.at[0])
-    keep.start()
     gather(2)
+    for at in range(1, NZ):
+        to_r[at].wait_recv()
+
+    def unpack_tokens(number, carry):
+        cut = pl.ds(pl.multiple_of(number * width, width), width)
+        token_grads[:, cut] = (
+            jnp.dot(
+                unpicks[PARTS],
+                returned[:, :, cut].reshape(count, width),
+                preferred_element_type=f32,
+            )
+            + jnp.dot(
+                unpicks[number],
+                returned[:, :, tail].reshape(count, width),
+                preferred_element_type=f32,
+            )
+        ).astype(bf16)
+        return carry
+
+    lax.fori_loop(0, PARTS, unpack_tokens, 0)
     for m in range(3):
         finish(m)
-    keep.wait()
     for at in range(NZ):
         to_e[at].wait_send()
         to_p[at].wait_send()
@@ -393,30 +512,35 @@
             copy.wait_send()
         if at:
             to_z[at].wait_send()
-            to_r[at].wait()
+            to_r[at].wait_send()
     to_partner.wait_send()
     for copy in to_y + to_g + to_s + to_b + to_t:
         copy.wait_send()
 
 
-def expert_step(slabs, owned):
-    _, _, _, long = slabs.shape
-    _, stored, width = owned.shape
-    features = NY * width
+def expert_step(tokens, cotangent, routes, codes, scales):
+    count, features = tokens.shape
+    _, stored, width = codes.shape
+    long = features + width
     units, half = 2 * stored, stored // 2
     dma = pltpu.SemaphoreType.DMA
     return pl.pallas_call(
         expert_kernel,
         out_shape=(
-            jax.ShapeDtypeStruct((NZ, MAIN, long), bf16),
+            jax.ShapeDtypeStruct((count, features), bf16),
             jax.ShapeDtypeStruct((3, stored, width), f32),
         ),
-        in_specs=[HBM, HBM],
-        out_specs=(HBM, VMEM),
+        in_specs=[HBM, HBM, VMEM, VMEM, VMEM],
+        out_specs=(VMEM, VMEM),
         scratch_shapes=[
+            pltpu.VMEM((NZ, 2, MAIN, long), bf16),
+            pltpu.VMEM((3, stored, width), bf16),
+            pltpu.VMEM((NZ, MAIN, long), bf16),
+            pltpu.VMEM((PARTS + 1, count, count), bf16),
+            pltpu.VMEM((PARTS + 1, count, count), bf16),
             pltpu.VMEM((2, NZ, ROWS, long), bf16),
             pltpu.VMEM((3, 2, stored, features), bf16),
-            pltpu.VMEM((3, 5 * ROWS, units), f32),
+            pltpu.VMEM((3, NZ * ROWS, units), f32),
             pltpu.VMEM((3, NZ * ROWS, units), bf16),
             pltpu.VMEM((NZ, 4, MAIN, long), bf16),
             pltpu.VMEM((5, 4 * MAIN, width), f32),
@@ -437,71 +561,24 @@
         + [dma((3,))] * 2
         + [dma((3, NY))] * 4
         + [dma((3,))] * 2
-        + [dma((2,))],
+        + [dma((2,))] * 2,
         compiler_params=pltpu.CompilerParams(
-            collective_id=0, has_side_effects=True, vmem_limit_bytes=60 << 20
+            collective_id=0, has_side_effects=True, vmem_limit_bytes=62 << 20
         ),
         cost_estimate=pl.CostEstimate(flops=10 * 10**9, bytes_accessed=10**8, transcendentals=0),
         name="expert_step",
-    )(slabs, owned)
+    )(
+        tokens.reshape(2, 4, MAIN, features),
+        cotangent.reshape(2, 4, MAIN, features),
+        routes.reshape(1, count),
+        codes,
+        scales,
+    )
 
 
 def shards(tokens, cotangent, routes, codes, scales, first_moment, second_moment):
-    row_count, features = tokens.shape
-    stored, width = codes.shape[1:]
-    _, z, _, _ = place()
     owned_full = codes.astype(f32) * jnp.repeat(scales, QB, axis=2)
-    owned = owned_full.astype(bf16)
-
-    route_ids = routes[:, 0]
-    matches = route_ids[:, None] == jnp.arange(NZ, dtype=jnp.int32)[None, :]
-    counted = matches.astype(jnp.int32)
-    earlier = jnp.cumsum(counted, axis=0) - counted
-    position = jnp.sum(jnp.where(matches, earlier, 0), axis=1)
-    ahead = (route_ids - z + NZ) % NZ
-    main_slot = jnp.where(position < MAIN, ahead * MAIN + position, -1)
-
-    def rest_slot(part):
-        return jnp.where(position < MAIN, -1, ahead * MAIN + part * REST + position - MAIN)
-
-    slots = jnp.arange(NZ * MAIN, dtype=jnp.int32)
-
-    def pack(values):
-        main = jnp.dot(
-            (slots[:, None] == main_slot[None, :]).astype(bf16), values, preferred_element_type=f32
-        )
-        chosen = jnp.concatenate(
-            [slots[:, None] == rest_slot(part)[None, :] for part in range(PARTS)], axis=1
-        ).astype(bf16)
-        quarters = jnp.concatenate(
-            [values[:, part * width : (part + 1) * width] for part in range(PARTS)], axis=0
-        )
-        rest = jnp.dot(chosen, quarters, preferred_element_type=f32)
-        packed = jnp.concatenate([main.astype(bf16), rest.astype(bf16)], axis=1)
-        return packed.reshape(NZ, MAIN, features + width)
-
-    slabs = jnp.stack([pack(tokens), pack(cotangent)], axis=1)
-    returned, gradient = expert_step(slabs, owned)
-    flat = returned.reshape(NZ * MAIN, features + width)
-    grad_tokens = jnp.concatenate(
-        [
-            jnp.dot(
-                jnp.concatenate(
-                    [
-                        main_slot[:, None] == slots[None, :],
-                        rest_slot(part)[:, None] == slots[None, :],
-                    ],
-                    axis=1,
-                ).astype(bf16),
-                jnp.concatenate(
-                    [flat[:, part * width : (part + 1) * width], flat[:, features:]], axis=0
-                ),
-                preferred_element_type=f32,
-            ).astype(bf16)
-            for part in range(PARTS)
-        ],
-        axis=1,
-    )
+    grad_tokens, gradient = expert_step(tokens, cotangent, routes, codes, scales)
     new_first = BETA_ONE * first_moment + (1.0 - BETA_ONE) * gradient
     new_second = BETA_TWO * second_moment + (1.0 - BETA_TWO) * gradient * gradient
     first_fix = 1.0 - BETA_ONE**STEP_COUNT

time: 189 us -> 173 us (0.915)
  other arithmetic: 13.4 us -> 5.29 us
  Pallas kernels: 167 us -> 163 us
  matrix products: 2.69 us -> 0 us
    pallas_call x1, Pallas kernels: 167 us -> 163 us  [expert_step(): pl.pallas_call(expert_kernel, out_shape=(jax.ShapeDtypeStruct((count, fea...]
    convert_element_type x2 -> x0, other arithmetic: 2.85 us -> none  [the longest x1 2.12 us: shards(): owned = owned_full.astype(bf16)]
    dot_general x8 -> x0, matrix products: 2.69 us -> none  [the longest x4 1.02 us: shards(): jnp.dot(jnp.concatenate([main_slot[:, None] == slots[None, :], rest_slot(...]
    another operation x2 -> x0, other arithmetic: 2.15 us -> none  [the longest x1 1.97 us: shards(): slabs = jnp.stack([pack(tokens), pack(cotangent)], axis=1)]
where the time goes in v4:
time: 173 us
  Pallas kernels  163 us (94%)
  other arithmetic  5.29 us (3%)
  local copies, waits for them, and re-layouts  4.25 us (2%)
    pallas_call x1, Pallas kernels, expert_step(): pl.pallas_call(expert_kernel, out_shape=(jax.ShapeDtypeStruct((count, fea...  163 us
    sub x1, other arithmetic, shards(): owned_full - LEARNING_RATE * (new_first / first_fix) / (jnp.sqrt(new_seco...  5.29 us

profile of v4, /device:TPU:1, one launch (start us, length us, event | category | flops | bytes accessed | tf_op | source)
XLA Modules:
  0.0 173.0 jit_solution(2914751014783886024)
XLA Ops:
  0.6 0.7 copy.14
  1.4 1.5 copy.13.scales
  2.9 0.1 broadcast_in_dim.3
  3.0 0.8 copy.15
  3.8 162.8 %expert_step.1 = (bf16[128,5120]{1,0:T(8,128)(2,1)}, f32[3,96,1280]{2,1,0:T(8,128)}) custom-call(bf16[2,4,16,5120]{3,2,1,0:T(8,128)(2,1)} %bitcast.5, bf16[2,4,16,5120]{3,2,1,0:T(8,128)(2,1)} %bitcast.6, s32[1,128]{1,0:T(1,128)} %bitcast.7, bf16[3,96,1280]{2,1,0:T(8,128)(2,1)} %codes.1, f32[3,96,10]{2,1,0:T(8,128)} %copy.13.scales), custom_call_target="tpu_custom_call" | custom-call | flops 10000000000 | bytes 100000000 | tf_op jit(solution)/shard_map/expert_step/pallas_call | solution.py:527
  166.7 0.0 copy-start
  166.7 5.3 %divide_subtract_fusion = (f32[3,96,1280]{2,1,0:T(8,128)}, f32[3,96,1280]{2,1,0:T(8,128)}, f32[3,96,1280]{2,1,0:T(8,128)}) fusion(f32[3,96,1280]{2,1,0:T(8,128)S(1)} %copy.15, bf16[3,96,1280]{2,1,0:T(8,128)(2,1)} %codes.1, f32[3,96,1280]{2,1,0:T(8,128)} %get-tuple-element.7, f32[3,96,1280]{2,1,0:T(8,128)} %param.12, f32[3,96,1280]{2,1,0:T(8,128)} %param.13), kind=kLoop, calls=%fused_computation.2 | loop fusion | flops 5160960 | bytes 11059200 | tf_op jit(solution)/shard_map/sub | solution.py:586
  172.0 0.0 copy-done
  172.0 1.1 copy.17
Async XLA Ops:
  166.7 5.3 %copy-start = (bf16[128,5120]{1,0:T(8,128)(2,1)S(1)}, bf16[128,5120]{1,0:T(8,128)(2,1)}, u32[]{:S(2)}) copy-start(bf16[128,5120]{1,0:T(8,128)(2,1)} %get-tuple-element.15) | copy-start | bytes 3932164

commit v5 on v4

--- a/solution.py
+++ b/solution.py
@@ -12,6 +12,7 @@
 MAIN, REST = 16, 4
 PARTS = 4
 ROWS = 4 * CAP
+NEXT = (1, 3)
 ORDER = (0, 1, 7, 2, 6, 3, 5, 4)
 HBM = pl.BlockSpec(memory_space=pltpu.HBM)
 VMEM = pl.BlockSpec(memory_space=pltpu.VMEM)
@@ -74,12 +75,12 @@
 
 
 def expert_kernel(
-    tokens, cotangent, routes, codes, scales, token_grads, gradient,
+    tokens, cotangent, routes, codes, scales, token_grads, gradient, full,
     slabs, owned, returned, picks, unpicks, inbound, weights, pre, signals, terms, rest, grads, crossed, paired,
-    from_x, block, from_y, from_y_block, part, given,
+    from_x, block, far_y, far_block, from_y, from_y_block, part, given,
     z_send, z_recv, x_send, x_recv, c_send, c_recv, w_send, w_recv,
     e_send, e_recv, p_send, p_recv, r_send, r_recv,
-    g_send, g_recv, y_send, y_recv, b_send, b_recv, t_send, t_recv, local, load,
+    g_send, g_recv, f_send, f_recv, h_send, h_recv, y_send, y_recv, b_send, b_recv, t_send, t_recv, local, load,
 ):
     y = lax.axis_index("group")
     stored, width = owned.shape[1:]
@@ -114,9 +115,12 @@
             )
         )
         loads[t].start()
-    for b in range(scales.shape[2]):
-        cut = pl.ds(b * QB, QB)
-        owned[:, :, cut] = (codes[:, :, cut].astype(f32) * scales[:, :, b : b + 1]).astype(bf16)
+    for m in range(3):
+        columned = scales[m].T
+        for b in range(scales.shape[1]):
+            cut = pl.ds(b * QB, QB)
+            full[m, :, cut] = codes[m, :, cut].astype(f32) * columned[:, b : b + 1]
+            owned[m, :, cut] = full[m, :, cut].astype(bf16)
 
     count = routes.shape[1]
     _, z, _, _ = place()
@@ -130,37 +134,37 @@
     position = jnp.sum(jnp.where(matches, earlier, 0.0), axis=0, keepdims=True).astype(jnp.int32)
     first_slot = (routes[...] - z + NZ) % NZ * MAIN
     in_main = position < MAIN
-    for number in range(PARTS + 1):
-        if number < PARTS:
-            slot = jnp.where(in_main, -1, first_slot + number * REST + position - MAIN)
-        else:
-            slot = jnp.where(in_main, first_slot + position, -1)
+    main = jnp.where(row_range == jnp.where(in_main, first_slot + position, -1), 1.0, 0.0)
+    unpicks[PARTS] = main.T.astype(bf16)
+    for number in range(PARTS):
+        slot = jnp.where(in_main, -1, first_slot + number * REST + position - MAIN)
         pick = jnp.where(row_range == slot, 1.0, 0.0)
-        picks[number] = pick.astype(bf16)
+        picks[number, :count] = main.astype(bf16)
+        picks[number, count:] = pick.astype(bf16)
         unpicks[number] = pick.T.astype(bf16)
 
     pl.semaphore_wait(barrier, len(peers))
 
-    to_partner = remote(owned, weights.at[:, 1, :, mine], w_send.at[0], w_recv.at[0], weight_pair())
+    to_partner = remote(
+        owned, weights.at[:, 1, :, mine], w_send.at[2 * NY], w_recv.at[2 * NY], weight_pair()
+    )
     keep_weights = pltpu.make_async_copy(owned, weights.at[:, 0, :, mine], local.at[1])
     keep_weights.start()
-    to_y = [
-        remote(owned, weights.at[:, 0, :, mine], w_send.at[k], w_recv.at[k], along_y(k))
-        for k in range(1, NY)
-    ]
+    to_y = {
+        (0, k): remote(owned, weights.at[:, 0, :, mine], w_send.at[k], w_recv.at[k], along_y(k))
+        for k in NEXT
+    }
     for t in range(2):
         loads[t].wait()
 
         def pack(number, carry):
             cut = pl.ds(pl.multiple_of(number * width, width), width)
             values = terms[2 * t : 2 * t + 2, :, :, cut].reshape(count, width)
-            slabs[:, t, :, cut] = (
-                jnp.dot(picks[PARTS], values, preferred_element_type=f32)
-                .astype(bf16)
-                .reshape(NZ, MAIN, width)
-            )
-            left = jnp.dot(picks[number], values, preferred_element_type=f32)
-            slabs[:, t, :, tail] = slabs[:, t, :, tail] + left.astype(bf16).reshape(NZ, MAIN, width)
+            packed = jnp.dot(
+                picks[number], values, preferred_element_type=f32
+            ).astype(bf16)
+            slabs[:, t, :, cut] = packed[:count].reshape(NZ, MAIN, width)
+            slabs[:, t, :, tail] = slabs[:, t, :, tail] + packed[count:].reshape(NZ, MAIN, width)
             return carry
 
         slabs[:, t, :, tail] = jnp.zeros((NZ, MAIN, width), bf16)
@@ -226,16 +230,21 @@
 
     def weights_on():
         to_partner.wait_recv()
-        for k in range(1, NY):
-            to_y.append(
-                remote(
-                    weights.at[:, 1, :, mine],
-                    weights.at[:, 1, :, mine],
-                    w_send.at[NY - 1 + k],
-                    w_recv.at[NY - 1 + k],
-                    along_y(k),
-                )
-            )
+        for k in NEXT:
+            to_y[1, k] = remote(
+                weights.at[:, 1, :, mine],
+                weights.at[:, 1, :, mine],
+                w_send.at[NY + k],
+                w_recv.at[NY + k],
+                along_y(k),
+            )
+
+    def relay(b):
+        for way, k in enumerate(NEXT):
+            to_y[b, k].wait_recv()
+            passed = weights.at[:, b, (low, high)[way], columns(NY - k)]
+            at = b * NY + 2 * way
+            to_y[b, 2, way] = remote(passed, passed, w_send.at[at], w_recv.at[at], along_y(k))
 
     def unpack_rest(first, count):
         for at in range(first, first + count):
@@ -260,12 +269,16 @@
         for k in turns:
             cut = columns(NY - k)
             for m in range(3):
-                term = lax.dot_general(
-                    inbound[m // 2, first : first + count, :, cut].reshape(rows, width),
-                    weights[m, :, :, cut].reshape(units, width),
-                    (((1,), (1,)), ((), ())),
-                    preferred_element_type=f32,
-                )
+                left = inbound[m // 2, first : first + count, :, cut].reshape(rows, width)
+                right = weights[m, :, :, cut].reshape(units, width)
+                if count > 2:
+                    term = lax.dot_general(
+                        left, right, (((1,), (1,)), ((), ())), preferred_element_type=f32
+                    )
+                else:
+                    term = lax.dot_general(
+                        right, left, (((1,), (1,)), ((), ())), preferred_element_type=f32
+                    ).T
                 if k == 0:
                     pre[m, stretch] = term
                 else:
@@ -320,10 +333,11 @@
                 )
 
     def weights_of(k):
-        if k:
-            to_y[k - 1].wait_recv()
-            to_y[NY - 2 + k].wait_recv()
-        else:
+        if k == 2:
+            for b in range(2):
+                for way in range(2):
+                    to_y[b, 2, way].wait_recv()
+        elif k == 0:
             keep_weights.wait()
 
     to_e, to_p, to_r = {}, {}, {}
@@ -349,7 +363,12 @@
                 terms.at[at, 0], returned.at[k], r_send.at[at], r_recv.at[at], along_z(NZ - k)
             )
 
-    to_g, to_s, to_b, to_t = [], [], [], []
+    to_g, to_f, to_h, to_s, to_b, to_t = [], [], [], [], [], []
+
+    def half_columns(k, way):
+        start = (y + k) % NY * width + way * (width // 2)
+        return pl.ds(pl.multiple_of(start, width // 2), width // 2)
+
 
     def differentiate(m):
         def columns_of(number, carry):
@@ -370,38 +389,72 @@
         to_g.append(
             remote(grads.at[m, 1, high], from_x.at[m], g_send.at[m], g_recv.at[m], weight_pair())
         )
-        for k in range(1, NY):
+        for way in range(2):
+            to_f.append(
+                remote(
+                    grads.at[m, :, low, half_columns(2, way)],
+                    far_y.at[way, m],
+                    f_send.at[m, way],
+                    f_recv.at[m, way],
+                    along_y(NEXT[way]),
+                )
+            )
+
+    def near(m):
+        for way in range(2):
+            to_f[2 * m + way].wait_recv()
+            cut = half_columns(NEXT[way], way)
+            grads[m, :, low, cut] = (
+                grads[m, :, low, cut].astype(f32) + far_y[way, m].astype(f32)
+            ).astype(bf16)
             to_s.append(
                 remote(
-                    grads.at[m, :, low, columns(k)],
-                    from_y.at[k - 1, m],
-                    y_send.at[m, k],
-                    y_recv.at[m, k],
-                    along_y(k),
+                    grads.at[m, :, low, columns(NEXT[way])],
+                    from_y.at[way, m],
+                    y_send.at[m, way],
+                    y_recv.at[m, way],
+                    along_y(NEXT[way]),
                 )
             )
 
     def through(m):
         to_g[m].wait_recv()
         block[m] = (grads[m, 0, high].astype(f32) + from_x[m].astype(f32)).astype(bf16)
-        for k in range(1, NY):
+        for way in range(2):
+            to_h.append(
+                remote(
+                    block.at[m, :, half_columns(2, way)],
+                    far_block.at[way, m],
+                    h_send.at[m, way],
+                    h_recv.at[m, way],
+                    along_y(NEXT[way]),
+                )
+            )
+
+    def near_block(m):
+        for way in range(2):
+            to_h[2 * m + way].wait_recv()
+            cut = half_columns(NEXT[way], way)
+            block[m, :, cut] = (
+                block[m, :, cut].astype(f32) + far_block[way, m].astype(f32)
+            ).astype(bf16)
             to_b.append(
                 remote(
-                    block.at[m, :, columns(k)],
-                    from_y_block.at[k - 1, m],
-                    b_send.at[m, k],
-                    b_recv.at[m, k],
-                    along_y(k),
+                    block.at[m, :, columns(NEXT[way])],
+                    from_y_block.at[way, m],
+                    b_send.at[m, way],
+                    b_recv.at[m, way],
+                    along_y(NEXT[way]),
                 )
             )
 
     def gather(m):
-        for copy in to_s[m * (NY - 1) : (m + 1) * (NY - 1)]:
+        for copy in to_s[2 * m : 2 * m + 2]:
             copy.wait_recv()
         for b in (1, 0):
             total = grads[m, b, low, mine].astype(f32)
-            for k in range(NY - 1):
-                total = total + from_y[k, m, b].astype(f32)
+            for way in range(2):
+                total = total + from_y[way, m, b].astype(f32)
             if b:
                 part[m] = total.astype(bf16)
                 to_t.append(
@@ -411,11 +464,11 @@
                 gradient[m, low] = total
 
     def finish(m):
-        for copy in to_b[m * (NY - 1) : (m + 1) * (NY - 1)]:
+        for copy in to_b[2 * m : 2 * m + 2]:
             copy.wait_recv()
         total = block[m, :, mine].astype(f32)
-        for k in range(NY - 1):
-            total = total + from_y_block[k, m].astype(f32)
+        for way in range(2):
+            total = total + from_y_block[way, m].astype(f32)
         gradient[m, high] = total
         to_t[m].wait_recv()
         gradient[m, low] = gradient[m, low] + given[m].astype(f32)
@@ -428,12 +481,14 @@
     arrive(2)
     launch(6)
     weights_on()
+    relay(0)
     cross(1)
     cross(2)
     arrive(3)
     launch(7)
     arrive(4)
     cross(3)
+    relay(1)
     cross(4)
     unpack_rest(0, 5)
     weights_of(0)
@@ -457,31 +512,43 @@
     activate(5, 2)
     give_back(5, 2, 0, 4)
     cross(7)
+    fold(6)
+    fold(5)
     unpack_rest(7, 1)
     project(7, 1, (0, 1, 3, 2))
     activate(7, 1)
-    FAR = (6, 5, 7, 4, 3, 2, 1, 0)
-    for at in (6, 5):
-        fold(at)
-    for m in range(3):
-        differentiate(m)
+    differentiate(0)
+    back(6)
+    differentiate(1)
+    back(5)
+    differentiate(2)
     give_back(7, 1, 0, 4)
-    for at in FAR[2:]:
-        fold(at)
-    back(FAR[0])
-    back(FAR[1])
+    fold(4)
+    fold(3)
+    fold(7)
+    near(0)
+    near(1)
+    near(2)
+    back(4)
+    fold(2)
+    fold(1)
+    back(3)
+    fold(0)
     through(0)
-    back(FAR[2])
+    back(7)
+    near_block(0)
+    back(2)
     gather(0)
-    back(FAR[3])
+    back(1)
     through(1)
-    back(FAR[4])
+    near_block(1)
     gather(1)
-    back(FAR[5])
-    back(FAR[6])
+    back(0)
     through(2)
-    back(FAR[7])
     gather(2)
+    near_block(2)
+    finish(0)
+    finish(1)
     for at in range(1, NZ):
         to_r[at].wait_recv()
 
@@ -502,8 +569,7 @@
         return carry
 
     lax.fori_loop(0, PARTS, unpack_tokens, 0)
-    for m in range(3):
-        finish(m)
+    finish(2)
     for at in range(NZ):
         to_e[at].wait_send()
         to_p[at].wait_send()
@@ -514,7 +580,7 @@
             to_z[at].wait_send()
             to_r[at].wait_send()
     to_partner.wait_send()
-    for copy in to_y + to_g + to_s + to_b + to_t:
+    for copy in list(to_y.values()) + to_g + to_f + to_h + to_s + to_b + to_t:
         copy.wait_send()
 
 
@@ -529,14 +595,15 @@
         out_shape=(
             jax.ShapeDtypeStruct((count, features), bf16),
             jax.ShapeDtypeStruct((3, stored, width), f32),
+            jax.ShapeDtypeStruct((3, stored, width), f32),
         ),
         in_specs=[HBM, HBM, VMEM, VMEM, VMEM],
-        out_specs=(VMEM, VMEM),
+        out_specs=(VMEM, VMEM, VMEM),
         scratch_shapes=[
             pltpu.VMEM((NZ, 2, MAIN, long), bf16),
             pltpu.VMEM((3, stored, width), bf16),
             pltpu.VMEM((NZ, MAIN, long), bf16),
-            pltpu.VMEM((PARTS + 1, count, count), bf16),
+            pltpu.VMEM((PARTS, 2 * count, count), bf16),
             pltpu.VMEM((PARTS + 1, count, count), bf16),
             pltpu.VMEM((2, NZ, ROWS, long), bf16),
             pltpu.VMEM((3, 2, stored, features), bf16),
@@ -549,17 +616,19 @@
             pltpu.VMEM((NZ, MAIN, long), bf16),
             pltpu.VMEM((3, half, features), bf16),
             pltpu.VMEM((3, half, features), bf16),
-            pltpu.VMEM((NY - 1, 3, 2, half, width), bf16),
-            pltpu.VMEM((NY - 1, 3, half, width), bf16),
+            pltpu.VMEM((2, 3, 2, half, width // 2), bf16),
+            pltpu.VMEM((2, 3, half, width // 2), bf16),
+            pltpu.VMEM((2, 3, 2, half, width), bf16),
+            pltpu.VMEM((2, 3, half, width), bf16),
             pltpu.VMEM((3, half, width), bf16),
             pltpu.VMEM((3, half, width), bf16),
         ]
         + [dma((NZ,))] * 4
         + [dma((2, NZ))] * 2
-        + [dma((2 * NY - 1,))] * 2
+        + [dma((2 * NY + 1,))] * 2
         + [dma((NZ,))] * 6
         + [dma((3,))] * 2
-        + [dma((3, NY))] * 4
+        + [dma((3, 2))] * 8
         + [dma((3,))] * 2
         + [dma((2,))] * 2,
         compiler_params=pltpu.CompilerParams(
@@ -572,13 +641,12 @@
         cotangent.reshape(2, 4, MAIN, features),
         routes.reshape(1, count),
         codes,
-        scales,
+        scales.transpose(0, 2, 1),
     )
 
 
 def shards(tokens, cotangent, routes, codes, scales, first_moment, second_moment):
-    owned_full = codes.astype(f32) * jnp.repeat(scales, QB, axis=2)
-    grad_tokens, gradient = expert_step(tokens, cotangent, routes, codes, scales)
+    grad_tokens, gradient, owned_full = expert_step(tokens, cotangent, routes, codes, scales)
     new_first = BETA_ONE * first_moment + (1.0 - BETA_ONE) * gradient
     new_second = BETA_TWO * second_moment + (1.0 - BETA_TWO) * gradient * gradient
     first_fix = 1.0 - BETA_ONE**STEP_COUNT

time: 173 us -> 166 us (0.960)
  Pallas kernels: 163 us -> 158 us
  local copies, waits for them, and re-layouts: 4.25 us -> 2.4 us
    pallas_call x1, Pallas kernels: 163 us -> 158 us  [expert_step(): pl.pallas_call(expert_kernel, out_shape=(jax.ShapeDtypeStruct((count, fea...]
where the time goes in v5:
time: 166 us
  Pallas kernels  158 us (95%)
  other arithmetic  4.99 us (3%)
  local copies, waits for them, and re-layouts  2.4 us (1%)
    pallas_call x1, Pallas kernels, expert_step(): pl.pallas_call(expert_kernel, out_shape=(jax.ShapeDtypeStruct((count, fea...  158 us
    sub x1, other arithmetic, shards(): owned_full - LEARNING_RATE * (new_first / first_fix) / (jnp.sqrt(new_seco...  4.99 us

profile of v5, /device:TPU:1, one launch (start us, length us, event | category | flops | bytes accessed | tf_op | source)
XLA Modules:
  0.0 166.3 jit_solution(10926084278175056586)
XLA Ops:
  0.6 1.3 copy.13
  2.0 0.0 copy-start
  2.0 158.2 %expert_step.1 = (bf16[128,5120]{1,0:T(8,128)(2,1)}, f32[3,96,1280]{2,1,0:T(8,128)}, f32[3,96,1280]{2,1,0:T(8,128)}) custom-call(bf16[2,4,16,5120]{3,2,1,0:T(8,128)(2,1)} %bitcast.7, bf16[2,4,16,5120]{3,2,1,0:T(8,128)(2,1)} %bitcast.8, s32[1,128]{1,0:T(1,128)} %bitcast.9, bf16[3,96,1280]{2,1,0:T(8,128)(2,1)} %codes.1, f32[3,10,96]{2,1,0:T(8,128)} %bitcast.6), custom_call_target="tpu_custom_call" | custom-call | flops 10000000000 | bytes 100000000 | tf_op jit(solution)/shard_map/expert_step/pallas_call | solution.py:593
  160.2 0.0 copy-done
  160.2 0.0 copy-start.1
  160.2 5.0 %divide_subtract_fusion = (f32[3,96,1280]{2,1,0:T(8,128)}, f32[3,96,1280]{2,1,0:T(8,128)}, f32[3,96,1280]{2,1,0:T(8,128)}) fusion(f32[3,96,1280]{2,1,0:T(8,128)} %get-tuple-element.8, f32[3,96,1280]{2,1,0:T(8,128)} %get-tuple-element.9, f32[3,96,1280]{2,1,0:T(8,128)S(1)} %copy-done, f32[3,96,1280]{2,1,0:T(8,128)} %param.13), kind=kLoop, calls=%fused_computation.2 | loop fusion | flops 4423680 | bytes 10321920 | tf_op jit(solution)/shard_map/sub | solution.py:654
  165.2 0.0 copy-done.1
  165.2 1.1 copy.15
Async XLA Ops:
  2.0 158.3 %copy-start = (f32[3,96,1280]{2,1,0:T(8,128)S(1)}, f32[3,96,1280]{2,1,0:T(8,128)}, u32[]{:S(2)}) copy-start(f32[3,96,1280]{2,1,0:T(8,128)} %param.12) | copy-start | bytes 4423684
  160.2 5.0 %copy-start.1 = (bf16[128,5120]{1,0:T(8,128)(2,1)S(1)}, bf16[128,5120]{1,0:T(8,128)(2,1)}, u32[]{:S(2)}) copy-start(bf16[128,5120]{1,0:T(8,128)(2,1)} %get-tuple-element.17) | copy-start | bytes 3932164

commit v6 on v5

--- a/solution.py
+++ b/solution.py
@@ -525,9 +525,9 @@
     give_back(7, 1, 0, 4)
     fold(4)
     fold(3)
-    fold(7)
     near(0)
     near(1)
+    fold(7)
     near(2)
     back(4)
     fold(2)

time: 166 us -> 166 us (level)
  no operation moved by 1% of the time
where the time goes in v6:
time: 166 us
  Pallas kernels  158 us (95%)
  other arithmetic  4.99 us (3%)
  local copies, waits for them, and re-layouts  2.4 us (1%)
    pallas_call x1, Pallas kernels, expert_step(): pl.pallas_call(expert_kernel, out_shape=(jax.ShapeDtypeStruct((count, fea...  158 us
    sub x1, other arithmetic, shards(): owned_full - LEARNING_RATE * (new_first / first_fix) / (jnp.sqrt(new_seco...  4.99 us

profile of v6, /device:TPU:1, one launch (start us, length us, event | category | flops | bytes accessed | tf_op | source)
XLA Modules:
  0.0 166.3 jit_solution(6648338106354043815)
XLA Ops:
  0.6 1.3 copy.13
  2.0 0.0 copy-start
  2.0 158.2 %expert_step.1 = (bf16[128,5120]{1,0:T(8,128)(2,1)}, f32[3,96,1280]{2,1,0:T(8,128)}, f32[3,96,1280]{2,1,0:T(8,128)}) custom-call(bf16[2,4,16,5120]{3,2,1,0:T(8,128)(2,1)} %bitcast.7, bf16[2,4,16,5120]{3,2,1,0:T(8,128)(2,1)} %bitcast.8, s32[1,128]{1,0:T(1,128)} %bitcast.9, bf16[3,96,1280]{2,1,0:T(8,128)(2,1)} %codes.1, f32[3,10,96]{2,1,0:T(8,128)} %bitcast.6), custom_call_target="tpu_custom_call" | custom-call | flops 10000000000 | bytes 100000000 | tf_op jit(solution)/shard_map/expert_step/pallas_call | solution.py:593
  160.2 0.0 copy-done
  160.2 0.0 copy-start.1
  160.2 5.0 %divide_subtract_fusion = (f32[3,96,1280]{2,1,0:T(8,128)}, f32[3,96,1280]{2,1,0:T(8,128)}, f32[3,96,1280]{2,1,0:T(8,128)}) fusion(f32[3,96,1280]{2,1,0:T(8,128)} %get-tuple-element.8, f32[3,96,1280]{2,1,0:T(8,128)} %get-tuple-element.9, f32[3,96,1280]{2,1,0:T(8,128)S(1)} %copy-done, f32[3,96,1280]{2,1,0:T(8,128)} %param.13), kind=kLoop, calls=%fused_computation.2 | loop fusion | flops 4423680 | bytes 10321920 | tf_op jit(solution)/shard_map/sub | solution.py:654
  165.2 0.0 copy-done.1
  165.2 1.1 copy.15
Async XLA Ops:
  2.0 158.3 %copy-start = (f32[3,96,1280]{2,1,0:T(8,128)S(1)}, f32[3,96,1280]{2,1,0:T(8,128)}, u32[]{:S(2)}) copy-start(f32[3,96,1280]{2,1,0:T(8,128)} %param.12) | copy-start | bytes 4423684
  160.2 5.0 %copy-start.1 = (bf16[128,5120]{1,0:T(8,128)(2,1)S(1)}, bf16[128,5120]{1,0:T(8,128)(2,1)}, u32[]{:S(2)}) copy-start(bf16[128,5120]{1,0:T(8,128)(2,1)} %get-tuple-element.17) | copy-start | bytes 3932164
